TPU v7x, 32 devices: a whole 2x2x4 slice. The times are simulated.
32 devices in a mesh: group: 2 (over x), gx: 16 (over z, y, core).
Axes of the slice: x: 2, y: 2, z: 4, core: 2. Of those that a mesh axis runs over, the one named last changes fastest.
Arguments:
- value: float32 [512, 64, 256], P(('group', 'gx')), parts along dimension 0, may hold values from -6 to 6
- drift: float32 [3, 512, 64, 256], P(None, ('group', 'gx')), parts along dimension 1, may hold values from -4 to 4
- gain: float32 [3, 512, 64, 256], P(None, ('group', 'gx')), parts along dimension 1, may hold values from -1 to 1
- target: int32 [512, 64, 256], P(('group', 'gx')), parts along dimension 0, may hold values 0 or 1
- obstacle: int32 [512, 64, 256], P(('group', 'gx')), parts along dimension 0, may hold values 0 or 1
Outputs:
- value_next: float32 [512, 64, 256], P(('group', 'gx')), parts along dimension 0
There are 2 independent parts, one for each index of `group`. A program takes and returns all parts, laid end to end along the dimension named above; each array names one. Nothing has to cross between parts.
All inputs are finite; a program needn't handle non-finite values. No bound on the sum of `target` or of `obstacle` on one device may be relied on, other than what follows from the above.
Results may differ from a plain program's by a relative error of at most 0.00002.
Values sent between devices are 32-bit elements; how exact they have to be, the bound alone decides.
No kernel may reach another device: no remote copies, remote signals or barrier semaphores. Data moves between devices by JAX's collectives and lax.ppermute only.
A program may use at most 128 MiB of HBM per device.

v0:
```python
import jax
import jax.numpy as jnp
from jax import lax
from jax.sharding import PartitionSpec as P


def padded_2(cells, sides, width):
    for axis, dim in sides:
        count = lax.axis_size(axis)
        ends = count - 1
        head = lax.slice_in_dim(cells, 0, width, axis=dim)
        tail = lax.slice_in_dim(cells, cells.shape[dim] - width, cells.shape[dim], axis=dim)
        cells = jnp.concatenate(
            [
                lax.ppermute(tail, axis, [(i, (i + 1) % count) for i in range(ends)]),
                cells,
                lax.ppermute(head, axis, [((i + 1) % count, i) for i in range(ends)]),
            ],
            axis=dim,
        )
    return cells


def weno(first, second, third, fourth, fifth):
    cand_a = first / 3.0 - 7.0 * second / 6.0 + 11.0 * third / 6.0
    cand_b = -second / 6.0 + 5.0 * third / 6.0 + fourth / 3.0
    cand_c = third / 3.0 + 5.0 * fourth / 6.0 - fifth / 6.0
    smooth_a = (
        13.0 / 12.0 * (first - 2.0 * second + third) ** 2
        + 0.25 * (first - 4.0 * second + 3.0 * third) ** 2
    )
    smooth_b = 13.0 / 12.0 * (second - 2.0 * third + fourth) ** 2 + 0.25 * (second - fourth) ** 2
    smooth_c = (
        13.0 / 12.0 * (third - 2.0 * fourth + fifth) ** 2
        + 0.25 * (3.0 * third - 4.0 * fourth + fifth) ** 2
    )
    weight_a = 0.1 / (1e-06 + smooth_a) ** 2
    weight_b = 0.6 / (1e-06 + smooth_b) ** 2
    weight_c = 0.3 / (1e-06 + smooth_c) ** 2
    return (weight_a * cand_a + weight_b * cand_b + weight_c * cand_c) / (
        weight_a + weight_b + weight_c
    )


def weno_pair(padded, axis):
    cells = padded.shape[axis] - 6
    diffs = jnp.diff(padded, axis=axis)

    def take(start):
        return lax.slice_in_dim(diffs, start, start + cells, axis=axis)

    minus = weno(take(0), take(1), take(2), take(3), take(4))
    plus = weno(take(5), take(4), take(3), take(2), take(1))
    return (minus, plus)


def rate(extended, fields):
    core = extended[3:-3]
    pad_y = jnp.pad(core, ((0, 0), (3, 3), (0, 0)), mode="edge")
    pad_z = jnp.pad(core, ((0, 0), (0, 0), (3, 3)), mode="wrap")
    mx, px = weno_pair(extended, 0)
    my, py = weno_pair(pad_y, 1)
    mz, pz = weno_pair(pad_z, 2)
    minus_list = (mx, my, mz)
    plus_list = (px, py, pz)
    along = jnp.zeros_like(core)
    control = jnp.zeros_like(core)
    damping = jnp.zeros_like(core)
    for comp in range(3):
        central = 0.5 * (minus_list[comp] + plus_list[comp])
        along = along + fields[comp] * central
        control = control + fields[3 + comp] * central
        damping = damping + (jnp.abs(fields[comp]) + jnp.abs(fields[3 + comp])) * 0.5 * (
            plus_list[comp] - minus_list[comp]
        )
    return -(along + jnp.abs(control) - damping)


def constrain(field, fields):
    field = jnp.where(fields[7] > 0.5, jnp.maximum(field, 1.0), field)
    return jnp.where(fields[6] > 0.5, jnp.minimum(field, -1.0), field)


def fix_edges(extended, width, is_first, is_last):
    length = extended.shape[0]
    lower = jnp.where(
        is_first,
        jnp.broadcast_to(extended[width : width + 1], extended[:width].shape),
        extended[:width],
    )
    upper = jnp.where(
        is_last,
        jnp.broadcast_to(
            extended[length - width - 1 : length - width], extended[length - width :].shape
        ),
        extended[length - width :],
    )
    return jnp.concatenate([lower, extended[width : length - width], upper], axis=0)


def shards(value, drift, gain, target, obstacle):
    place = lax.axis_index("gx")
    is_first = place == 0
    is_last = place == lax.axis_size("gx") - 1
    speed = jnp.sum(jnp.abs(drift) + jnp.abs(gain), axis=0)
    step_size = 0.5 / lax.pmax(jnp.max(speed), "gx")
    fields = jnp.concatenate(
        [drift, gain, target.astype(jnp.float32)[None], obstacle.astype(jnp.float32)[None]], axis=0
    )

    def advance(field):
        extended = padded_2(field, (("gx", 0),), 3)
        extended = fix_edges(extended, 3, is_first, is_last)
        return field + step_size * rate(extended, fields)

    first = constrain(advance(value), fields)
    second = constrain(0.75 * value + 0.25 * advance(first), fields)
    return constrain(value / 3.0 + 2.0 / 3.0 * advance(second), fields)


def solution(mesh):
    placed = (
        P(("group", "gx"), None, None),
        P(None, ("group", "gx"), None, None),
        P(None, ("group", "gx"), None, None),
        P(("group", "gx"), None, None),
        P(("group", "gx"), None, None),
    )
    return jax.shard_map(
        shards,
        mesh=mesh,
        in_specs=placed,
        out_specs=P(("group", "gx"), None, None),
        check_vma=False,
    )
```

profile of v0, /device:TPU:1, one launch (start us, length us, event | category | flops | bytes accessed | tf_op | source)
XLA Modules:
  0.0 138.3 jit_solution(17475759209021914323)
XLA Ops:
  0.0 1.8 %copy.29 = f32[16,64,256]{2,0,1:T(8,128)S(1)} copy(f32[16,64,256]{2,1,0:T(8,128)} %param.5) | data formatting | bytes 2097152 | tf_op args[0]
  1.8 0.0 copy-start
  1.9 0.0 copy-start.9
  1.9 0.9 fusion.12
  2.7 4.7 %collective-permute-start = (f32[3,64,256]{2,0,1:T(4,128)}, f32[3,64,256]{2,0,1:T(4,128)}, u32[]{:S(2)}, u32[]{:S(2)}) collective-permute-start(f32[3,64,256]{2,0,1:T(4,128)} %get-tuple-element.32), channel_id=1, source_target_pairs={{0,1},{1,2},{2,3},{3,4},{4,5},{5,6},{6,7},{7,8},{8,9},{9,10},{10,1... | collective-permute-start | bytes 589832 | tf_op jit(solution)/shard_map/ppermute | solution.py:15
  7.4 1.9 %collective-permute-start.1 = (f32[3,64,256]{2,0,1:T(4,128)}, f32[3,64,256]{2,0,1:T(4,128)S(1)}, u32[]{:S(2)}, u32[]{:S(2)}) collective-permute-start(f32[3,64,256]{2,0,1:T(4,128)} %get-tuple-element.33), channel_id=1, source_target_pairs={{1,0},{2,1},{3,2},{4,3},{5,4},{6,5},{7,6},{8,7},{9,8},{10,9},{11,1... | collective-permute-start | bytes 589832 | tf_op jit(solution)/shard_map/ppermute | solution.py:17
  9.4 1.1 fusion.13
  10.5 3.0 %add_reduce_fusion = f32[16,64,256]{2,1,0:T(8,128)S(1)} fusion(f32[3,16,64,256]{3,2,1,0:T(8,128)S(1)} %copy-done.9, f32[3,16,64,256]{3,2,1,0:T(8,128)} %param.6), kind=kLoop, calls=%fused_computation | loop fusion | flops 2883584 | bytes 7340032 | tf_op jit(solution)/shard_map/reduce_sum | solution.py:105
  13.5 2.7 %fusion.4 = (f32[1,16,64,256]{3,2,1,0:T(8,128)}, f32[1,16,64,256]{3,2,1,0:T(8,128)}, f32[1,16,64,256]{3,2,1,0:T(8,128)}, f32[1,16,64,256]{3,2,1,0:T(8,128)}, f32...) fusion(f32[3,16,64,256]{3,2,1,0:T(8,128)S(1)} %copy-done.9, f32[3,16,64,256]{3,2,1,0:T(8,128)S(1)} %copy-done.10), kind=kLoop, calls=%fused_computation.56 | loop fusion | bytes 12582912 | tf_op jit(solution)/shard_map/slice | solution.py:72
  16.3 0.1 pad_maximum_fusion.6
  16.4 0.1 slice_subtract_fusion.8
  16.5 0.9 reduce_max.9
  17.4 30.3 %pmax.7 = f32[]{:T(128)} all-reduce(f32[]{:T(128)} %reduce_max.9), channel_id=1, replica_groups=mesh['group'=2,'gx'=16] {'gx'}, use_global_device_ids=true, to_apply=%region_2.0 | all-reduce | flops 1 | bytes 8 | tf_op jit(solution)/shard_map/pmax | solution.py:106
  47.7 1.8 %pad_maximum_fusion.1 = f32[16,64,262]{2,0,1:T(8,128)S(1)} fusion(f32[16,64,3]{2,0,1:T(8,128)} %get-tuple-element.37, f32[16,64,256]{2,0,1:T(8,128)S(1)} %copy.29, f32[16,64,3]{2,0,1:T(8,128)} %get-tuple-element.36), kind=kLoop, calls=%fused_computation.8 | loop fusion | flops 536576 | bytes 2146304 | tf_op jit(solution)/shard_map/jit(_pad)/concatenate | solution.py:60
  49.5 0.5 slice_subtract_fusion.4
  50.7 0.0 copy-start.1
  50.7 1.0 slice_bitcast_fusion.1
  51.7 0.0 collective-permute-done
  51.7 1.0 broadcast_select_fusion.5
  52.7 0.1 broadcast_select_fusion.4
  52.8 0.3 pad_maximum_fusion
  53.1 0.0 copy-start.2
  53.1 0.2 slice_subtract_fusion.5
  53.3 0.7 copy-done.6
  54.0 0.3 copy-done.7
  54.3 0.3 copy-done.8
  54.7 0.4 copy-done.2
  55.0 0.3 copy-done.3
  55.4 0.3 copy-done.4
  55.7 0.3 copy-done.5
  56.0 21.2 %minimum_select_fusion.2 = (f32[16,64,256]{2,0,1:T(8,128)S(1)}, pred[16,64,256]{2,0,1:T(8,128)(4,1)S(1)}, pred[16,64,256]{2,0,1:T(8,128)(4,1)S(1)}) fusion(f32[16,64,261]{2,0,1:T(8,128)S(1)} %slice_subtract_fusion.4, f32[16,69,256]{2,0,1:T(8,128)S(1)} %slice_subtract_fusion.8, f32[21,64,256]{2,0,1:T(8,128)S(1)} %slice_subtract_fusion.5, ...), kind=kLoop, calls=%fused_computation.17 | loop fusion | flops 110624768 | bytes 29884420 | tf_op jit(solution)/shard_map/jit(_where)/select_n | solution.py:81
  77.2 0.1 fusion.9
  77.3 0.1 fusion.10
  77.4 0.2 fusion.11
  77.6 1.9 %collective-permute-start.2 = (f32[3,64,256]{2,0,1:T(4,128)S(1)}, f32[3,64,256]{2,0,1:T(4,128)S(1)}, u32[]{:S(2)}, u32[]{:S(2)}) collective-permute-start(f32[3,64,256]{2,0,1:T(4,128)S(1)} %get-tuple-element.24), channel_id=1, source_target_pairs={{0,1},{1,2},{2,3},{3,4},{4,5},{5,6},{6,7},{7,8},{8,9},{9,10},{10,1... | collective-permute-start | bytes 589832 | tf_op jit(solution)/shard_map/ppermute | solution.py:15
  79.6 4.0 %collective-permute-start.3 = (f32[3,64,256]{2,0,1:T(4,128)S(1)}, f32[3,64,256]{2,0,1:T(4,128)S(1)}, u32[]{:S(2)}, u32[]{:S(2)}) collective-permute-start(f32[3,64,256]{2,0,1:T(4,128)S(1)} %get-tuple-element.25), channel_id=1, source_target_pairs={{1,0},{2,1},{3,2},{4,3},{5,4},{6,5},{7,6},{8,7},{9,8},{10,9},{11,1... | collective-permute-start | bytes 589832 | tf_op jit(solution)/shard_map/ppermute | solution.py:17
  83.6 0.6 pad_maximum_fusion.3
  84.2 0.5 slice_subtract_fusion.2
  84.7 0.1 pad_maximum_fusion.7
  84.8 0.1 slice_subtract_fusion.7
  84.9 0.8 collective-permute-done.2
  85.7 0.1 broadcast_select_fusion.3
  85.8 1.5 %collective-permute-done.3 = f32[3,64,256]{2,0,1:T(4,128)S(1)} collective-permute-done((f32[3,64,256]{2,0,1:T(4,128)S(1)}, f32[3,64,256]{2,0,1:T(4,128)S(1)}, u32[]{:S(2)}, u32[]{:S(2)}) %collective-permute-start.3) | collective-permute-done | bytes 196640 | tf_op jit(solution)/shard_map/ppermute | solution.py:17
  87.3 0.1 broadcast_select_fusion.2
  87.3 0.3 pad_maximum_fusion.2
  87.6 0.2 slice_subtract_fusion.3
  87.8 18.7 %minimum_select_fusion.1 = f32[16,64,256]{2,0,1:T(8,128)S(1)} fusion(pred[16,64,256]{2,0,1:T(8,128)(4,1)S(1)} %get-tuple-element.7, pred[16,64,256]{2,0,1:T(8,128)(4,1)S(1)} %get-tuple-element.6, f32[16,64,256]{2,0,1:T(8,128)S(1)} %get-tuple-element.5, f32[16,64,261]{2,0,1:T(8,128)S(1)} %slice_subtract_fusion.2, f32[16,69,256]{2,0,1:T(8,128)S(1)} %slice_subtract_fusion.7, ...), kind=kLoop, calls=%fused_computation.15 | loop fusion | flops 110362624 | bytes 28835844 | tf_op jit(solution)/shard_map/jit(_where)/select_n | solution.py:81
  106.5 0.1 fusion.6
  106.6 0.1 fusion.7
  106.7 0.2 fusion.8
  106.9 2.9 %collective-permute-start.4 = (f32[3,64,256]{2,0,1:T(4,128)S(1)}, f32[3,64,256]{2,0,1:T(4,128)S(1)}, u32[]{:S(2)}, u32[]{:S(2)}) collective-permute-start(f32[3,64,256]{2,0,1:T(4,128)S(1)} %get-tuple-element.16), channel_id=1, source_target_pairs={{0,1},{1,2},{2,3},{3,4},{4,5},{5,6},{6,7},{7,8},{8,9},{9,10},{10,1... | collective-permute-start | bytes 589832 | tf_op jit(solution)/shard_map/ppermute | solution.py:15
  109.8 1.9 %collective-permute-start.5 = (f32[3,64,256]{2,0,1:T(4,128)S(1)}, f32[3,64,256]{2,0,1:T(4,128)S(1)}, u32[]{:S(2)}, u32[]{:S(2)}) collective-permute-start(f32[3,64,256]{2,0,1:T(4,128)S(1)} %get-tuple-element.17), channel_id=1, source_target_pairs={{1,0},{2,1},{3,2},{4,3},{5,4},{6,5},{7,6},{8,7},{9,8},{10,9},{11,1... | collective-permute-start | bytes 589832 | tf_op jit(solution)/shard_map/ppermute | solution.py:17
  111.7 0.6 pad_maximum_fusion.5
  112.3 0.5 slice_subtract_fusion
  112.9 0.1 pad_maximum_fusion.8
  112.9 0.1 slice_subtract_fusion.6
  113.1 2.9 %collective-permute-done.4 = f32[3,64,256]{2,0,1:T(4,128)S(1)} collective-permute-done((f32[3,64,256]{2,0,1:T(4,128)S(1)}, f32[3,64,256]{2,0,1:T(4,128)S(1)}, u32[]{:S(2)}, u32[]{:S(2)}) %collective-permute-start.4) | collective-permute-done | bytes 196640 | tf_op jit(solution)/shard_map/ppermute | solution.py:15
  115.9 0.1 broadcast_select_fusion.1
  116.0 1.5 %collective-permute-done.5 = f32[3,64,256]{2,0,1:T(4,128)S(1)} collective-permute-done((f32[3,64,256]{2,0,1:T(4,128)S(1)}, f32[3,64,256]{2,0,1:T(4,128)S(1)}, u32[]{:S(2)}, u32[]{:S(2)}) %collective-permute-start.5) | collective-permute-done | bytes 196640 | tf_op jit(solution)/shard_map/ppermute | solution.py:17
  117.5 0.1 broadcast_select_fusion
  117.6 0.3 pad_maximum_fusion.4
  117.8 0.2 slice_subtract_fusion.1
  118.0 18.7 %minimum_select_fusion = f32[16,64,256]{2,0,1:T(8,128)S(1)} fusion(pred[16,64,256]{2,0,1:T(8,128)(4,1)S(1)} %get-tuple-element.7, pred[16,64,256]{2,0,1:T(8,128)(4,1)S(1)} %get-tuple-element.6, f32[16,64,256]{2,0,1:T(8,128)S(1)} %minimum_select_fusion.1, f32[16,64,261]{2,0,1:T(8,128)S(1)} %slice_subtract_fusion, f32[16,69,256]{2,0,1:T(8,128)S(1)} %slice_subtract_fusion.6, ...), kind=kLoop, calls=%fused_computation.13 | loop fusion | flops 110362624 | bytes 28835844 | tf_op jit(solution)/shard_map/jit(_where)/select_n | solution.py:81
  136.7 1.6 %copy.47 = f32[16,64,256]{2,1,0:T(8,128)} copy(f32[16,64,256]{2,0,1:T(8,128)S(1)} %minimum_select_fusion) | data formatting | bytes 2097152 | tf_op jit(solution)/shard_map/jit(_where)/select_n | solution.py:81
  (25 shorter events, 0.1 us)
Async XLA Ops:
  1.8 45.9 %copy-start = (f32[16,64,256]{2,0,1:T(8,128)}, f32[16,64,256]{2,0,1:T(8,128)S(1)}, u32[]{:S(2)}) copy-start(f32[16,64,256]{2,0,1:T(8,128)S(1)} %copy.29) | copy-start | bytes 3145732
  1.9 8.6 %copy-start.9 = (f32[3,16,64,256]{3,2,1,0:T(8,128)S(1)}, f32[3,16,64,256]{3,2,1,0:T(8,128)}, u32[]{:S(2)}) copy-start(f32[3,16,64,256]{3,2,1,0:T(8,128)} %param.7) | copy-start | bytes 9437188
  2.7 48.9 %collective-permute-start = (f32[3,64,256]{2,0,1:T(4,128)}, f32[3,64,256]{2,0,1:T(4,128)}, u32[]{:S(2)}, u32[]{:S(2)}) collective-permute-start(f32[3,64,256]{2,0,1:T(4,128)} %get-tuple-element.32), channel_id=1, source_target_pairs={{0,1},{1,2},{2,3},{3,4},{4,5},{5,6},{6,7},{7,8},{8,9},{9,10},{10,1... | collective-permute-start | bytes 589832 | tf_op jit(solution)/shard_map/ppermute | solution.py:15
  7.4 45.3 %collective-permute-start.1 = (f32[3,64,256]{2,0,1:T(4,128)}, f32[3,64,256]{2,0,1:T(4,128)S(1)}, u32[]{:S(2)}, u32[]{:S(2)}) collective-permute-start(f32[3,64,256]{2,0,1:T(4,128)} %get-tuple-element.33), channel_id=1, source_target_pairs={{1,0},{2,1},{3,2},{4,3},{5,4},{6,5},{7,6},{8,7},{9,8},{10,9},{11,1... | collective-permute-start | bytes 589832 | tf_op jit(solution)/shard_map/ppermute | solution.py:17
  10.5 3.0 %copy-start.10 = (f32[3,16,64,256]{3,2,1,0:T(8,128)S(1)}, f32[3,16,64,256]{3,2,1,0:T(8,128)}, u32[]{:S(2)}) copy-start(f32[3,16,64,256]{3,2,1,0:T(8,128)} %param.6) | copy-start | bytes 9437188
  50.7 2.1 %copy-start.1 = (f32[16,64,256]{2,0,1:T(8,128)S(1)}, f32[16,64,256]{2,0,1:T(8,128)}, u32[]{:S(2)}) copy-start(f32[16,64,256]{2,0,1:T(8,128)} %copy-done) | copy-start | bytes 3145732
  52.8 1.2 copy-start.6
  52.8 1.5 %copy-start.7 = (f32[1,16,64,256]{3,2,1,0:T(8,128)S(1)}, f32[1,16,64,256]{3,2,1,0:T(8,128)}, u32[]{:S(2)}) copy-start(f32[1,16,64,256]{3,2,1,0:T(8,128)} %get-tuple-element.39) | copy-start | bytes 3145732
  52.8 1.8 %copy-start.8 = (f32[1,16,64,256]{3,2,1,0:T(8,128)S(1)}, f32[1,16,64,256]{3,2,1,0:T(8,128)}, u32[]{:S(2)}) copy-start(f32[1,16,64,256]{3,2,1,0:T(8,128)} %get-tuple-element.40) | copy-start | bytes 3145732
  53.1 2.0 %copy-start.2 = (f32[16,64,256]{2,1,0:T(8,128)S(1)}, f32[16,64,256]{2,1,0:T(8,128)}, u32[]{:S(2)}) copy-start(f32[16,64,256]{2,1,0:T(8,128)} %param.5) | copy-start | bytes 3145732
  53.1 2.3 %copy-start.3 = (f32[1,16,64,256]{3,2,1,0:T(8,128)S(1)}, f32[1,16,64,256]{3,2,1,0:T(8,128)}, u32[]{:S(2)}) copy-start(f32[1,16,64,256]{3,2,1,0:T(8,128)} %get-tuple-element.8) | copy-start | bytes 3145732
  53.1 2.6 %copy-start.4 = (f32[1,16,64,256]{3,2,1,0:T(8,128)S(1)}, f32[1,16,64,256]{3,2,1,0:T(8,128)}, u32[]{:S(2)}) copy-start(f32[1,16,64,256]{3,2,1,0:T(8,128)} %get-tuple-element.9) | copy-start | bytes 3145732
  53.1 2.9 %copy-start.5 = (f32[1,16,64,256]{3,2,1,0:T(8,128)S(1)}, f32[1,16,64,256]{3,2,1,0:T(8,128)}, u32[]{:S(2)}) copy-start(f32[1,16,64,256]{3,2,1,0:T(8,128)} %get-tuple-element.10) | copy-start | bytes 3145732
  77.6 8.0 %collective-permute-start.2 = (f32[3,64,256]{2,0,1:T(4,128)S(1)}, f32[3,64,256]{2,0,1:T(4,128)S(1)}, u32[]{:S(2)}, u32[]{:S(2)}) collective-permute-start(f32[3,64,256]{2,0,1:T(4,128)S(1)} %get-tuple-element.24), channel_id=1, source_target_pairs={{0,1},{1,2},{2,3},{3,4},{4,5},{5,6},{6,7},{7,8},{8,9},{9,10},{10,1... | collective-permute-start | bytes 589832 | tf_op jit(solution)/shard_map/ppermute | solution.py:15
  79.6 7.7 %collective-permute-start.3 = (f32[3,64,256]{2,0,1:T(4,128)S(1)}, f32[3,64,256]{2,0,1:T(4,128)S(1)}, u32[]{:S(2)}, u32[]{:S(2)}) collective-permute-start(f32[3,64,256]{2,0,1:T(4,128)S(1)} %get-tuple-element.25), channel_id=1, source_target_pairs={{1,0},{2,1},{3,2},{4,3},{5,4},{6,5},{7,6},{8,7},{9,8},{10,9},{11,1... | collective-permute-start | bytes 589832 | tf_op jit(solution)/shard_map/ppermute | solution.py:17
  106.9 9.0 %collective-permute-start.4 = (f32[3,64,256]{2,0,1:T(4,128)S(1)}, f32[3,64,256]{2,0,1:T(4,128)S(1)}, u32[]{:S(2)}, u32[]{:S(2)}) collective-permute-start(f32[3,64,256]{2,0,1:T(4,128)S(1)} %get-tuple-element.16), channel_id=1, source_target_pairs={{0,1},{1,2},{2,3},{3,4},{4,5},{5,6},{6,7},{7,8},{8,9},{9,10},{10,1... | collective-permute-start | bytes 589832 | tf_op jit(solution)/shard_map/ppermute | solution.py:15
  109.8 7.7 %collective-permute-start.5 = (f32[3,64,256]{2,0,1:T(4,128)S(1)}, f32[3,64,256]{2,0,1:T(4,128)S(1)}, u32[]{:S(2)}, u32[]{:S(2)}) collective-permute-start(f32[3,64,256]{2,0,1:T(4,128)S(1)} %get-tuple-element.17), channel_id=1, source_target_pairs={{1,0},{2,1},{3,2},{4,3},{5,4},{6,5},{7,6},{8,7},{9,8},{10,9},{11,1... | collective-permute-start | bytes 589832 | tf_op jit(solution)/shard_map/ppermute | solution.py:17
where the time goes:
time: 139 us; the launch traced here: 138 us
  other arithmetic  70.2 us (51%)
  blocking collectives  30.3 us (22%)
  starting transfers between devices  17.3 us (12%)
  local copies, waits for them, and re-layouts  12.7 us (9%)
  waiting for transfers between devices  6.71 us (5%)
    select_n x3, other arithmetic, constrain(): return jnp.where(fields[6] > 0.5, jnp.minimum(field, -1.0), field)  58.6 us
    pmax x1, blocking collectives, shards(): step_size = 0.5 / lax.pmax(jnp.max(speed), 'gx')  30.3 us
    ppermute x3, starting transfers between devices, padded_2(): lax.ppermute(tail, axis, [(i, (i + 1) % count) for i in range(ends)])  9.48 us
    ppermute x3, starting transfers between devices, padded_2(): lax.ppermute(head, axis, [((i + 1) % count, i) for i in range(ends)])  7.81 us
    unnamed x27, local copies, waits for them, and re-layouts  4.56 us
    ppermute x3, waiting for transfers between devices, padded_2(): lax.ppermute(tail, axis, [(i, (i + 1) % count) for i in range(ends)])  3.67 us
    reduce_sum x1, other arithmetic, shards(): speed = jnp.sum(jnp.abs(drift) + jnp.abs(gain), axis=0)  3.04 us
    ppermute x3, waiting for transfers between devices, padded_2(): lax.ppermute(head, axis, [((i + 1) % count, i) for i in range(ends)])  3.03 us
  transfers between devices with their start and end apart: 6, of which 4 were waited for; matrix products, arithmetic and copies ran while one was open for 11% of the time, Pallas kernels for 0%

commit v1 on v0

v1 whole, which is shorter than its diff:
```python
import functools

import jax
import jax.numpy as jnp
from jax import lax
from jax.experimental import pallas as pl
from jax.experimental.pallas import tpu as pltpu
from jax.sharding import PartitionSpec as P

LANES = 128
SUB = 8
APPROX = True


def rcp(x):
    return pl.reciprocal(x, approx=APPROX)


def twice_square(s):
    return (s + s) * s


def inverse_weights(t, g, left, right):
    base = t * t * (4.0 / 3.0) + 1e-6
    h = base - g
    m = base + g
    l = h + left
    r = h + right
    return rcp(r * r), rcp(l * l), rcp(m * m * (1.0 / 6.0))


def blend(alpha, beta, gamma, far, near):
    gamma = 3.0 * gamma
    return (alpha * far + gamma * near) * rcp(alpha + beta + gamma)


def prep_kernel(drift, gain, target, obstacle, fp, fm, lo, hi, top):
    step = pl.program_id(0)
    speed = None
    for k in range(3):
        a = drift[k]
        w = jnp.abs(a) + jnp.abs(gain[k])
        fp[k] = a - w
        fm[k] = a + w
        speed = w if speed is None else speed + w
    lo[...] = jnp.where(obstacle[...] == 1, 1.0, -jnp.inf)
    hi[...] = jnp.where(target[...] == 1, -1.0, jnp.inf)
    rows, ny, nz = speed.shape
    m = jnp.max(speed, axis=0)
    m = jnp.max(m.reshape(ny // SUB, SUB, nz), axis=0)
    best = m[:, :LANES]
    for c in range(1, nz // LANES):
        best = jnp.maximum(best, m[:, c * LANES:(c + 1) * LANES])

    @pl.when(step == 0)
    def _():
        top[...] = best

    @pl.when(step > 0)
    def _():
        top[...] = jnp.maximum(top[...], best)


def prep(drift, gain, target, obstacle, block):
    _, rows, ny, nz = drift.shape
    big = pl.BlockSpec((3, block, ny, nz), lambda i: (0, i, 0, 0))
    one = pl.BlockSpec((block, ny, nz), lambda i: (i, 0, 0))
    sds = jax.ShapeDtypeStruct
    f32 = jnp.float32
    return pl.pallas_call(
        prep_kernel,
        grid=(rows // block,),
        in_specs=[big, big, one, one],
        out_specs=[big, big, one, one, pl.BlockSpec((SUB, LANES), lambda i: (0, 0))],
        out_shape=[sds(drift.shape, f32)] * 2 + [sds(target.shape, f32)] * 2 + [sds((SUB, LANES), f32)],
        compiler_params=pltpu.CompilerParams(vmem_limit_bytes=32 << 20),
    )(drift, gain, target, obstacle)


def fill(pad, row, value, ny, halves):
    for h in range(halves):
        part = value[:, h * LANES:(h + 1) * LANES]
        pad[row, h, SUB:SUB + ny] = part
        pad[row, h, 0:SUB] = jnp.broadcast_to(part[0:1], (SUB, LANES))
        pad[row, h, SUB + ny:2 * SUB + ny] = jnp.broadcast_to(part[ny - 1:ny], (SUB, LANES))


def x_pass(pad, fp, fm, gain, ac, bb, rows, ny, halves):
    tiles = ny // SUB

    def body(i, _):
        h = i // tiles
        y = pl.multiple_of((i % tiles) * SUB, SUB)
        u = lambda r: pad[r, h, pl.ds(y + SUB, SUB), :]
        z = pl.multiple_of(h * LANES, LANES)
        d, s, p, t, q, q2, ir, il, im = ({} for _ in range(9))
        prev = u(0)
        for r in range(rows + 5):
            nxt = u(r + 1)
            d[r] = nxt - prev
            prev = nxt
            if r >= 1:
                s[r] = d[r] - d[r - 1]
                p[r] = twice_square(s[r])
            if r >= 2:
                k = r - 1
                t[k] = s[k + 1] - s[k]
                ir[k], il[k], im[k] = inverse_weights(t[k], s[k] * s[k + 1], p[k], p[k + 1])
                if k >= 2:
                    q[k] = t[k] - t[k - 1]
                    q2[k] = q[k] + q[k]
                c = k - 1
                if c >= 3:
                    minus = blend(ir[c - 2], im[c - 1], il[c], q2[c - 1], q[c])
                    plus = blend(il[c + 1], im[c], ir[c - 1], q2[c + 1], q[c])
                    mid = 3.0 * (d[c] + d[c - 1])
                    dm = mid - t[c - 1] - minus
                    dp = mid - t[c] + plus
                    x = c - 3
                    f = lambda a: a[0, x, pl.ds(y, SUB), pl.ds(z, LANES)]
                    ac[x, h, pl.ds(y, SUB), :] = f(fp) * dp + f(fm) * dm
                    bb[x, h, pl.ds(y, SUB), :] = f(gain) * (dp + dm)
        return 0

    lax.fori_loop(0, tiles * halves, body, 0)


def roll(parts, shift, lane):
    n = len(parts)
    turned = [pltpu.roll(v, shift % LANES, 1) for v in parts]
    if shift > 0:
        return [jnp.where(lane < shift, turned[(i - 1) % n], turned[i]) for i in range(n)]
    return [jnp.where(lane >= LANES + shift, turned[(i + 1) % n], turned[i]) for i in range(n)]


def each(f, *lists):
    return [f(*a) for a in zip(*lists)]


def z_part(u, lane):
    d = each(lambda a, b: a - b, roll(u, -1, lane), u)
    d1 = roll(d, 1, lane)
    s = each(lambda a, b: a - b, d, d1)
    mid = each(lambda a, b: 3.0 * (a + b), d, d1)
    s1 = roll(s, -1, lane)
    t = each(lambda a, b: a - b, s1, s)
    t1 = roll(t, 1, lane)
    q = each(lambda a, b: a - b, t, t1)
    q2 = each(lambda a: a + a, q)
    p = each(twice_square, s)
    g = each(lambda a, b: a * b, s, s1)
    base = each(lambda a: a * a * (4.0 / 3.0) + 1e-6, t)
    h = each(lambda a, b: a - b, base, g)
    im = each(lambda a, b: rcp((a + b) * (a + b) * (1.0 / 6.0)), base, g)
    il = each(lambda a, b: rcp((a + b) * (a + b)), h, p)
    ir1 = each(lambda a, b: rcp((a + b) * (a + b)), roll(h, 1, lane), p)
    minus = each(blend, roll(ir1, 1, lane), roll(im, 1, lane), il, roll(q2, 1, lane), q)
    plus = each(blend, roll(il, -1, lane), im, ir1, roll(q2, -1, lane), q)
    dm = each(lambda a, b, c: a - b - c, mid, t1, minus)
    dp = each(lambda a, b, c: a - b + c, mid, t, plus)
    return dm, dp


def y_stage(pad, x, h, work, ny):
    wt, wq, wr, wl, wm = work
    for k in range(ny // SUB + 1):
        a = 6 + SUB * k
        u0, u1, u2, u3 = (pad[x + 3, h, a + o:a + o + SUB, :] for o in (-1, 0, 1, 2))
        d0, d1, d2 = u1 - u0, u2 - u1, u3 - u2
        s0, s1 = d1 - d0, d2 - d1
        t = s1 - s0
        wt[h, a:a + SUB] = t
        r, l, m = inverse_weights(t, s0 * s1, twice_square(s0), twice_square(s1))
        wr[h, a:a + SUB] = r
        wl[h, a:a + SUB] = l
        wm[h, a:a + SUB] = m


def y_part(pad, x, h, work, tile):
    wt, wq, wr, wl, wm = work
    c = SUB + SUB * tile
    at = lambda w, o: w[h, c + o:c + o + SUB, :]
    t2, t1, t0, tn = (at(wt, o) for o in (-2, -1, 0, 1))
    q = t0 - t1
    qa = t1 - t2
    qb = tn - t0
    minus = blend(at(wr, -2), at(wm, -1), at(wl, 0), qa + qa, q)
    plus = blend(at(wl, 1), at(wm, 0), at(wr, -1), qb + qb, q)
    mid = 3.0 * (pad[x + 3, h, c + 1:c + 1 + SUB, :] - pad[x + 3, h, c - 1:c - 1 + SUB, :])
    return mid - t1 - minus, mid - t0 + plus


def yz_pass(pad, fp, fm, gain, ac, bb, work, rows, ny, halves, finish):
    tiles = ny // SUB

    def body(x, _):
        lane = lax.broadcasted_iota(jnp.int32, (SUB, LANES), 1)
        for h in range(halves):
            y_stage(pad, x, h, work, ny)
        for tile in range(tiles):
            y = tile * SUB
            u = [pad[x + 3, h, SUB + y:2 * SUB + y, :] for h in range(halves)]
            dm, dp = z_part(u, lane)
            for h in range(halves):
                ym, yp = y_part(pad, x, h, work, tile)
                f = lambda a, k: a[k, x, y:y + SUB, h * LANES:(h + 1) * LANES]
                total = ac[x, h, y:y + SUB, :] + f(fp, 1) * yp + f(fm, 1) * ym
                total = total + f(fp, 2) * dp[h] + f(fm, 2) * dm[h]
                control = bb[x, h, y:y + SUB, :] + f(gain, 1) * (yp + ym) + f(gain, 2) * (dp[h] + dm[h])
                finish(x, y, h, u[h], total + jnp.abs(control))
        return 0

    lax.fori_loop(0, rows, body, 0)


def stage_kernel(weights, first, u, below, above, ends, kappa, value, fp, fm, gain, lo, hi, out, pad, ac, bb, *work):
    rows, ny, nz = u.shape
    halves = nz // LANES
    for r in range(3):
        fill(pad, r, jnp.where(ends[0] == 1, u[0], below[r]), ny, halves)
        fill(pad, rows + 3 + r, jnp.where(ends[1] == 1, u[rows - 1], above[r]), ny, halves)

    def load(r, _):
        fill(pad, r + 3, u[r], ny, halves)
        return 0

    lax.fori_loop(0, rows, load, 0)
    x_pass(pad, fp, fm, gain, ac, bb, rows, ny, halves)

    def finish(x, y, h, mine, total):
        at = (x, slice(y, y + SUB), slice(h * LANES, (h + 1) * LANES))
        if first:
            out[at] = total
            return
        keep, take = weights
        new = keep * value[at] + take * mine - kappa[0] * total
        out[at] = jnp.minimum(jnp.maximum(new, lo[at]), hi[at])

    yz_pass(pad, fp, fm, gain, ac, bb, work, rows, ny, halves, finish)


def stage(weights, first, u, below, above, ends, kappa, value, fp, fm, gain, lo, hi):
    rows, ny, nz = u.shape
    halves = nz // LANES
    vm = pl.BlockSpec(memory_space=pltpu.VMEM)
    sm = pl.BlockSpec(memory_space=pltpu.SMEM)
    f32 = jnp.float32
    return pl.pallas_call(
        functools.partial(stage_kernel, weights, first),
        in_specs=[vm, vm, vm, sm, sm] + [vm] * 6,
        out_specs=vm,
        out_shape=jax.ShapeDtypeStruct(u.shape, f32),
        scratch_shapes=[
            pltpu.VMEM((rows + 6, halves, ny + 2 * SUB, LANES), f32),
            pltpu.VMEM((rows, halves, ny, LANES), f32),
            pltpu.VMEM((rows, halves, ny, LANES), f32),
        ] + [pltpu.VMEM((halves, ny + 2 * SUB, LANES), f32)] * 5,
        compiler_params=pltpu.CompilerParams(vmem_limit_bytes=32 << 20),
    )(u, below, above, ends, kappa, value, fp, fm, gain, lo, hi)


def neighbours(field, count):
    up = [(i, i + 1) for i in range(count - 1)]
    down = [(i + 1, i) for i in range(count - 1)]
    below = lax.ppermute(field[-3:], "gx", up)
    above = lax.ppermute(field[:3], "gx", down)
    return below, above


def shards(value, drift, gain, target, obstacle):
    count = lax.axis_size("gx")
    place = lax.axis_index("gx")
    ends = jnp.stack([place == 0, place == count - 1]).astype(jnp.int32)
    below, above = neighbours(value, count)
    fp, fm, lo, hi, top = prep(drift, gain, target, obstacle, 4)
    step = 1
    while step < count:
        top = jnp.maximum(top, lax.ppermute(top, "gx", [(i, i ^ step) for i in range(count)]))
        step *= 2
    kappa = (0.5 / jnp.max(top) / 12.0).reshape(1)
    total = stage((1.0, 0.0), True, value, below, above, ends, kappa, value, fp, fm, gain, lo, hi)
    one = jnp.minimum(jnp.maximum(value - kappa[0] * total, lo), hi)
    below, above = neighbours(one, count)
    two = stage((0.75, 0.25), False, one, below, above, ends, 0.25 * kappa, value, fp, fm, gain, lo, hi)
    below, above = neighbours(two, count)
    return stage((1 / 3, 2 / 3), False, two, below, above, ends, 2 / 3 * kappa, value, fp, fm, gain, lo, hi)


def solution(mesh):
    flat = P(("group", "gx"), None, None)
    deep = P(None, ("group", "gx"), None, None)
    return jax.shard_map(
        shards,
        mesh=mesh,
        in_specs=(flat, deep, deep, flat, flat),
        out_specs=flat,
        check_vma=False,
    )
```

time: 139 us -> 96.6 us (0.69)
  the two profiles are of different devices: /device:TPU:1 before, /device:TPU:16 now
where the time goes in v1:
time: 96.6 us; the launch traced here: 96 us
  Pallas kernels  37.5 us (39%)
  local copies, waits for them, and re-layouts  20.8 us (22%)
  waiting for transfers between devices  18.8 us (19%)
  starting transfers between devices  17 us (18%)
  other arithmetic  1.07 us (1%)
    pallas_call x3, Pallas kernels, stage(): pl.pallas_call(functools.partial(stage_kernel, weights, first), in_specs=...  35.6 us
    unnamed x28, local copies, waits for them, and re-layouts  18.9 us
    ppermute x3, waiting for transfers between devices, neighbours(): below = lax.ppermute(field[-3:], 'gx', up)  9.41 us
    ppermute x4, waiting for transfers between devices, shards(): lax.ppermute(top, 'gx', [(i, i ^ step) for i in range(count)])  7.34 us
    ppermute x3, starting transfers between devices, neighbours(): above = lax.ppermute(field[:3], 'gx', down)  6.73 us
    ppermute x3, starting transfers between devices, neighbours(): below = lax.ppermute(field[-3:], 'gx', up)  6.73 us
    ppermute x4, starting transfers between devices, shards(): lax.ppermute(top, 'gx', [(i, i ^ step) for i in range(count)])  3.51 us
    ppermute x3, waiting for transfers between devices, neighbours(): above = lax.ppermute(field[:3], 'gx', down)  2.02 us
  transfers between devices with their start and end apart: 10, of which 7 were waited for; matrix products, arithmetic and copies ran while one was open for 3% of the time, Pallas kernels for 0%

profile of v1, /device:TPU:16, one launch (start us, length us, event | category | flops | bytes accessed | tf_op | source)
XLA Modules:
  0.0 96.0 jit_solution(7326265334769449156)
XLA Ops:
  0.0 0.0 copy-start
  0.0 1.9 %copy-done = f32[3,16,64,256]{3,2,1,0:T(8,128)S(1)} copy-done((f32[3,16,64,256]{3,2,1,0:T(8,128)S(1)}, f32[3,16,64,256]{3,2,1,0:T(8,128)}, u32[]{:S(2)}) %copy-start) | copy-done | bytes 3145752
  1.9 0.0 copy-start.11
  1.9 1.9 %copy-done.11 = f32[3,16,64,256]{3,2,1,0:T(8,128)S(1)} copy-done((f32[3,16,64,256]{3,2,1,0:T(8,128)S(1)}, f32[3,16,64,256]{3,2,1,0:T(8,128)}, u32[]{:S(2)}) %copy-start.11) | copy-done | bytes 3145752
  3.8 0.0 copy-start.12
  3.8 1.2 %copy-done.12 = s32[16,64,256]{2,1,0:T(8,128)S(1)} copy-done((s32[16,64,256]{2,1,0:T(8,128)S(1)}, s32[16,64,256]{2,1,0:T(8,128)}, u32[]{:S(2)}) %copy-start.12) | copy-done | bytes 1048600
  5.0 0.0 copy-start.13
  5.0 1.2 %copy-done.13 = s32[16,64,256]{2,1,0:T(8,128)S(1)} copy-done((s32[16,64,256]{2,1,0:T(8,128)S(1)}, s32[16,64,256]{2,1,0:T(8,128)}, u32[]{:S(2)}) %copy-start.13) | copy-done | bytes 1048600
  6.2 0.0 copy-start.1
  6.2 1.9 %shard_map.55 = (f32[3,16,64,256]{3,2,1,0:T(8,128)S(1)}, f32[3,16,64,256]{3,2,1,0:T(8,128)S(1)}, f32[16,64,256]{2,1,0:T(8,128)S(1)}, f32[16,64,256]{2,1,0:T(8,128)S(1)}, f32[8,128]{1,0:T(8,128)S(1)}) custom-call(f32[3,16,64,256]{3,2,1,0:T(8,128)S(1)} %copy-done.11, f32[3,16,64,256]{3,2,1,0:T(8,128)S(1)} %copy-done, s32[16,64,256]{2,1,0:T(8,128)S(1)} %copy-done.12, ...), custom_call_target="tpu_custom_call" | custom-call | tf_op jit(solution)/shard_map/pallas_call | solution.py:70
  8.2 0.0 copy-start.3
  8.2 1.6 %copy-done.3 = f32[3,16,64,256]{3,2,1,0:T(8,128)} copy-done((f32[3,16,64,256]{3,2,1,0:T(8,128)}, f32[3,16,64,256]{3,2,1,0:T(8,128)S(1)}, u32[]{:S(2)}) %copy-start.3) | copy-done | bytes 3145752
  9.8 0.0 copy-start.5
  9.8 1.7 %copy-done.5 = f32[3,16,64,256]{3,2,1,0:T(8,128)} copy-done((f32[3,16,64,256]{3,2,1,0:T(8,128)}, f32[3,16,64,256]{3,2,1,0:T(8,128)S(1)}, u32[]{:S(2)}) %copy-start.5) | copy-done | bytes 3145752
  11.5 0.0 copy-start.7
  11.5 1.0 %copy-done.7 = f32[16,64,256]{2,1,0:T(8,128)} copy-done((f32[16,64,256]{2,1,0:T(8,128)}, f32[16,64,256]{2,1,0:T(8,128)S(1)}, u32[]{:S(2)}) %copy-start.7) | copy-done | bytes 1048600
  12.4 0.0 copy-start.9
  12.4 1.0 %copy-done.9 = f32[16,64,256]{2,1,0:T(8,128)} copy-done((f32[16,64,256]{2,1,0:T(8,128)}, f32[16,64,256]{2,1,0:T(8,128)S(1)}, u32[]{:S(2)}) %copy-start.9) | copy-done | bytes 1048600
  13.4 0.0 collective-permute-start
  13.4 1.2 %collective-permute-done = f32[8,128]{1,0:T(8,128)S(1)} collective-permute-done((f32[8,128]{1,0:T(8,128)S(1)}, f32[8,128]{1,0:T(8,128)S(1)}, u32[]{:S(2)}, u32[]{:S(2)}) %collective-permute-start) | collective-permute-done | bytes 4128 | tf_op jit(solution)/shard_map/ppermute | solution.py:278
  14.6 1.5 %collective-permute-start.1 = (f32[8,128]{1,0:T(8,128)S(1)}, f32[8,128]{1,0:T(8,128)S(1)}, u32[]{:S(2)}, u32[]{:S(2)}) collective-permute-start(f32[8,128]{1,0:T(8,128)S(1)} %max.15), channel_id=1, source_target_pairs={{0,2},{1,3},{2,0},{3,1},{4,6},{5,7},{6,4},{7,5},{8,10},{9,11},{10,... | collective-permute-start | bytes 12296 | tf_op jit(solution)/shard_map/ppermute | solution.py:278
  16.1 2.1 %collective-permute-done.1 = f32[8,128]{1,0:T(8,128)S(1)} collective-permute-done((f32[8,128]{1,0:T(8,128)S(1)}, f32[8,128]{1,0:T(8,128)S(1)}, u32[]{:S(2)}, u32[]{:S(2)}) %collective-permute-start.1) | collective-permute-done | bytes 4128 | tf_op jit(solution)/shard_map/ppermute | solution.py:278
  18.2 1.6 %collective-permute-start.2 = (f32[8,128]{1,0:T(8,128)S(1)}, f32[8,128]{1,0:T(8,128)S(1)}, u32[]{:S(2)}, u32[]{:S(2)}) collective-permute-start(f32[8,128]{1,0:T(8,128)S(1)} %max.16), channel_id=1, source_target_pairs={{0,4},{1,5},{2,6},{3,7},{4,0},{5,1},{6,2},{7,3},{8,12},{9,13},{10,... | collective-permute-start | bytes 12296 | tf_op jit(solution)/shard_map/ppermute | solution.py:278
  19.8 1.8 %fusion.2 = (f32[3,64,256]{2,1,0:T(8,128)}, f32[3,64,256]{2,1,0:T(8,128)}) fusion(f32[16,64,256]{2,1,0:T(8,128)} %value.5), kind=kLoop, calls=%fused_computation.5 | loop fusion | bytes 786432 | tf_op jit(solution)/shard_map/slice | solution.py:266
  21.5 1.9 %collective-permute-start.5 = (f32[3,64,256]{2,1,0:T(8,128)}, f32[3,64,256]{2,1,0:T(8,128)S(1)}, u32[]{:S(2)}, u32[]{:S(2)}) collective-permute-start(f32[3,64,256]{2,1,0:T(8,128)} %get-tuple-element.19), channel_id=1, source_target_pairs={{1,0},{2,1},{3,2},{4,3},{5,4},{6,5},{7,6},{8,7},{9,8},{10,9},{11,1... | collective-permute-start | bytes 589832 | tf_op jit(solution)/shard_map/ppermute | solution.py:266
  23.5 2.4 %collective-permute-start.4 = (f32[3,64,256]{2,1,0:T(8,128)}, f32[3,64,256]{2,1,0:T(8,128)S(1)}, u32[]{:S(2)}, u32[]{:S(2)}) collective-permute-start(f32[3,64,256]{2,1,0:T(8,128)} %get-tuple-element.20), channel_id=1, source_target_pairs={{0,1},{1,2},{2,3},{3,4},{4,5},{5,6},{6,7},{7,8},{8,9},{9,10},{10,1... | collective-permute-start | bytes 589832 | tf_op jit(solution)/shard_map/ppermute | solution.py:265
  25.9 0.0 collective-permute-done.2
  25.9 0.4 collective-permute-start.3
  26.3 0.1 add_convert_fusion.ends
  26.4 4.1 %collective-permute-done.3 = f32[8,128]{1,0:T(8,128)S(1)} collective-permute-done((f32[8,128]{1,0:T(8,128)S(1)}, f32[8,128]{1,0:T(8,128)S(1)}, u32[]{:S(2)}, u32[]{:S(2)}) %collective-permute-start.3) | collective-permute-done | bytes 4128 | tf_op jit(solution)/shard_map/ppermute | solution.py:278
  30.5 0.7 maximum_reduce_fusion
  31.9 0.0 collective-permute-done.5.above
  31.9 0.0 collective-permute-done.4.below
  31.9 0.0 copy-done.1
  31.9 0.0 copy-start.2
  31.9 1.2 %copy-done.2 = f32[16,64,256]{2,1,0:T(8,128)S(1)} copy-done((f32[16,64,256]{2,1,0:T(8,128)S(1)}, f32[16,64,256]{2,1,0:T(8,128)}, u32[]{:S(2)}) %copy-start.2) | copy-done | bytes 1048600
  33.1 0.0 copy-start.4
  33.1 1.9 %copy-done.4 = f32[3,16,64,256]{3,2,1,0:T(8,128)S(1)} copy-done((f32[3,16,64,256]{3,2,1,0:T(8,128)S(1)}, f32[3,16,64,256]{3,2,1,0:T(8,128)}, u32[]{:S(2)}) %copy-start.4) | copy-done | bytes 3145752
  35.0 0.0 copy-start.6
  35.0 1.9 %copy-done.6 = f32[3,16,64,256]{3,2,1,0:T(8,128)S(1)} copy-done((f32[3,16,64,256]{3,2,1,0:T(8,128)S(1)}, f32[3,16,64,256]{3,2,1,0:T(8,128)}, u32[]{:S(2)}) %copy-start.6) | copy-done | bytes 3145752
  36.9 0.0 copy-start.8
  36.9 1.2 %copy-done.8 = f32[16,64,256]{2,1,0:T(8,128)S(1)} copy-done((f32[16,64,256]{2,1,0:T(8,128)S(1)}, f32[16,64,256]{2,1,0:T(8,128)}, u32[]{:S(2)}) %copy-start.8) | copy-done | bytes 1048600
  38.1 0.0 copy-start.10
  38.1 1.2 %copy-done.10 = f32[16,64,256]{2,1,0:T(8,128)S(1)} copy-done((f32[16,64,256]{2,1,0:T(8,128)S(1)}, f32[16,64,256]{2,1,0:T(8,128)}, u32[]{:S(2)}) %copy-start.10) | copy-done | bytes 1048600
  39.4 11.4 %shard_map.56 = f32[16,64,256]{2,1,0:T(8,128)S(1)} custom-call(f32[16,64,256]{2,1,0:T(8,128)S(1)} %copy-done.2, f32[3,64,256]{2,1,0:T(8,128)S(1)} %collective-permute-done.4.below, f32[3,64,256]{2,1,0:T(8,128)S(1)} %collective-permute-done.5.above, s32[2]{0:T(128)S(1)} %add_convert_fusion.ends, f32[1]{0:T(128)} %bitcast.2.kappa, ...), custom_call_target="tpu_custom_call" | custom-call | tf_op jit(solution)/shard_map/pallas_call | solution.py:248
  50.7 0.3 maximum_minimum_fusion.u
  51.1 2.9 %collective-permute-start.7 = (f32[3,64,256]{2,1,0:T(8,128)S(1)}, f32[3,64,256]{2,1,0:T(8,128)S(1)}, u32[]{:S(2)}, u32[]{:S(2)}) collective-permute-start(f32[3,64,256]{2,1,0:T(8,128)S(1)} %get-tuple-element.17), channel_id=1, source_target_pairs={{1,0},{2,1},{3,2},{4,3},{5,4},{6,5},{7,6},{8,7},{9,8},{10,9},{11,1... | collective-permute-start | bytes 589832 | tf_op jit(solution)/shard_map/ppermute | solution.py:266
  54.0 1.9 %collective-permute-start.6 = (f32[3,64,256]{2,1,0:T(8,128)S(1)}, f32[3,64,256]{2,1,0:T(8,128)S(1)}, u32[]{:S(2)}, u32[]{:S(2)}) collective-permute-start(f32[3,64,256]{2,1,0:T(8,128)S(1)} %get-tuple-element.18), channel_id=1, source_target_pairs={{0,1},{1,2},{2,3},{3,4},{4,5},{5,6},{6,7},{7,8},{8,9},{9,10},{10,1... | collective-permute-start | bytes 589832 | tf_op jit(solution)/shard_map/ppermute | solution.py:265
  56.0 1.3 %collective-permute-done.7.above = f32[3,64,256]{2,1,0:T(8,128)S(1)} collective-permute-done((f32[3,64,256]{2,1,0:T(8,128)S(1)}, f32[3,64,256]{2,1,0:T(8,128)S(1)}, u32[]{:S(2)}, u32[]{:S(2)}) %collective-permute-start.7) | collective-permute-done | bytes 196640 | tf_op jit(solution)/shard_map/ppermute | solution.py:266
  57.2 4.7 %collective-permute-done.6.below = f32[3,64,256]{2,1,0:T(8,128)S(1)} collective-permute-done((f32[3,64,256]{2,1,0:T(8,128)S(1)}, f32[3,64,256]{2,1,0:T(8,128)S(1)}, u32[]{:S(2)}, u32[]{:S(2)}) %collective-permute-start.6) | collective-permute-done | bytes 196640 | tf_op jit(solution)/shard_map/ppermute | solution.py:265
  61.9 11.6 %shard_map.57.u = f32[16,64,256]{2,1,0:T(8,128)S(1)} custom-call(f32[16,64,256]{2,1,0:T(8,128)S(1)} %maximum_minimum_fusion.u, f32[3,64,256]{2,1,0:T(8,128)S(1)} %collective-permute-done.6.below, f32[3,64,256]{2,1,0:T(8,128)S(1)} %collective-permute-done.7.above, s32[2]{0:T(128)S(1)} %add_convert_fusion.ends, f32[1]{0:T(128)S(6)} %mul.14.kappa, ...), custom_call_target="tpu_custom_call" | custom-call | tf_op jit(solution)/shard_map/pallas_call | solution.py:248
  73.6 1.9 %collective-permute-start.9 = (f32[3,64,256]{2,1,0:T(8,128)S(1)}, f32[3,64,256]{2,1,0:T(8,128)S(1)}, u32[]{:S(2)}, u32[]{:S(2)}) collective-permute-start(f32[3,64,256]{2,1,0:T(8,128)S(1)} %get-tuple-element.15), channel_id=1, source_target_pairs={{1,0},{2,1},{3,2},{4,3},{5,4},{6,5},{7,6},{8,7},{9,8},{10,9},{11,1... | collective-permute-start | bytes 589832 | tf_op jit(solution)/shard_map/ppermute | solution.py:266
  75.5 2.4 %collective-permute-start.8 = (f32[3,64,256]{2,1,0:T(8,128)S(1)}, f32[3,64,256]{2,1,0:T(8,128)S(1)}, u32[]{:S(2)}, u32[]{:S(2)}) collective-permute-start(f32[3,64,256]{2,1,0:T(8,128)S(1)} %get-tuple-element.16), channel_id=1, source_target_pairs={{0,1},{1,2},{2,3},{3,4},{4,5},{5,6},{6,7},{7,8},{8,9},{9,10},{10,1... | collective-permute-start | bytes 589832 | tf_op jit(solution)/shard_map/ppermute | solution.py:265
  77.9 0.7 collective-permute-done.9.above
  78.7 4.7 %collective-permute-done.8.below = f32[3,64,256]{2,1,0:T(8,128)S(1)} collective-permute-done((f32[3,64,256]{2,1,0:T(8,128)S(1)}, f32[3,64,256]{2,1,0:T(8,128)S(1)}, u32[]{:S(2)}, u32[]{:S(2)}) %collective-permute-start.8) | collective-permute-done | bytes 196640 | tf_op jit(solution)/shard_map/ppermute | solution.py:265
  83.4 12.6 %shard_map.58 = f32[16,64,256]{2,1,0:T(8,128)} custom-call(f32[16,64,256]{2,1,0:T(8,128)S(1)} %shard_map.57.u, f32[3,64,256]{2,1,0:T(8,128)S(1)} %collective-permute-done.8.below, f32[3,64,256]{2,1,0:T(8,128)S(1)} %collective-permute-done.9.above, s32[2]{0:T(128)S(1)} %add_convert_fusion.ends, f32[1]{0:T(128)S(6)} %mul.15.kappa, ...), custom_call_target="tpu_custom_call" | custom-call | tf_op jit(solution)/shard_map/pallas_call | solution.py:248
  (5 shorter events, 0.1 us)
Async XLA Ops:
  0.0 1.9 %copy-start = (f32[3,16,64,256]{3,2,1,0:T(8,128)S(1)}, f32[3,16,64,256]{3,2,1,0:T(8,128)}, u32[]{:S(2)}) copy-start(f32[3,16,64,256]{3,2,1,0:T(8,128)} %gain.7) | copy-start | bytes 9437188
  1.9 1.9 %copy-start.11 = (f32[3,16,64,256]{3,2,1,0:T(8,128)S(1)}, f32[3,16,64,256]{3,2,1,0:T(8,128)}, u32[]{:S(2)}) copy-start(f32[3,16,64,256]{3,2,1,0:T(8,128)} %drift.1) | copy-start | bytes 9437188
  3.8 1.2 %copy-start.12 = (s32[16,64,256]{2,1,0:T(8,128)S(1)}, s32[16,64,256]{2,1,0:T(8,128)}, u32[]{:S(2)}) copy-start(s32[16,64,256]{2,1,0:T(8,128)} %target.1) | copy-start | bytes 3145732
  5.0 1.2 %copy-start.13 = (s32[16,64,256]{2,1,0:T(8,128)S(1)}, s32[16,64,256]{2,1,0:T(8,128)}, u32[]{:S(2)}) copy-start(s32[16,64,256]{2,1,0:T(8,128)} %obstacle.1) | copy-start | bytes 3145732
  6.2 25.7 %copy-start.1 = (f32[3,16,64,256]{3,2,1,0:T(8,128)S(1)}, f32[3,16,64,256]{3,2,1,0:T(8,128)}, u32[]{:S(2)}) copy-start(f32[3,16,64,256]{3,2,1,0:T(8,128)} %gain.7) | copy-start | bytes 9437188
  8.2 1.6 %copy-start.3 = (f32[3,16,64,256]{3,2,1,0:T(8,128)}, f32[3,16,64,256]{3,2,1,0:T(8,128)S(1)}, u32[]{:S(2)}) copy-start(f32[3,16,64,256]{3,2,1,0:T(8,128)S(1)} %get-tuple-element.11.fp) | copy-start | bytes 9437188
  9.8 1.7 %copy-start.5 = (f32[3,16,64,256]{3,2,1,0:T(8,128)}, f32[3,16,64,256]{3,2,1,0:T(8,128)S(1)}, u32[]{:S(2)}) copy-start(f32[3,16,64,256]{3,2,1,0:T(8,128)S(1)} %get-tuple-element.12.fm) | copy-start | bytes 9437188
  11.5 1.0 %copy-start.7 = (f32[16,64,256]{2,1,0:T(8,128)}, f32[16,64,256]{2,1,0:T(8,128)S(1)}, u32[]{:S(2)}) copy-start(f32[16,64,256]{2,1,0:T(8,128)S(1)} %get-tuple-element.13.lo) | copy-start | bytes 3145732
  12.4 1.0 %copy-start.9 = (f32[16,64,256]{2,1,0:T(8,128)}, f32[16,64,256]{2,1,0:T(8,128)S(1)}, u32[]{:S(2)}) copy-start(f32[16,64,256]{2,1,0:T(8,128)S(1)} %get-tuple-element.14.hi) | copy-start | bytes 3145732
  13.4 1.2 %collective-permute-start = (f32[8,128]{1,0:T(8,128)S(1)}, f32[8,128]{1,0:T(8,128)S(1)}, u32[]{:S(2)}, u32[]{:S(2)}) collective-permute-start(f32[8,128]{1,0:T(8,128)S(1)} %get-tuple-element.10), channel_id=1, source_target_pairs={{0,1},{1,0},{2,3},{3,2},{4,5},{5,4},{6,7},{7,6},{8,9},{9,8},{10,11... | collective-permute-start | bytes 12296 | tf_op jit(solution)/shard_map/ppermute | solution.py:278
  14.6 3.6 %collective-permute-start.1 = (f32[8,128]{1,0:T(8,128)S(1)}, f32[8,128]{1,0:T(8,128)S(1)}, u32[]{:S(2)}, u32[]{:S(2)}) collective-permute-start(f32[8,128]{1,0:T(8,128)S(1)} %max.15), channel_id=1, source_target_pairs={{0,2},{1,3},{2,0},{3,1},{4,6},{5,7},{6,4},{7,5},{8,10},{9,11},{10,... | collective-permute-start | bytes 12296 | tf_op jit(solution)/shard_map/ppermute | solution.py:278
  18.2 7.7 %collective-permute-start.2 = (f32[8,128]{1,0:T(8,128)S(1)}, f32[8,128]{1,0:T(8,128)S(1)}, u32[]{:S(2)}, u32[]{:S(2)}) collective-permute-start(f32[8,128]{1,0:T(8,128)S(1)} %max.16), channel_id=1, source_target_pairs={{0,4},{1,5},{2,6},{3,7},{4,0},{5,1},{6,2},{7,3},{8,12},{9,13},{10,... | collective-permute-start | bytes 12296 | tf_op jit(solution)/shard_map/ppermute | solution.py:278
  21.5 10.3 %collective-permute-start.5 = (f32[3,64,256]{2,1,0:T(8,128)}, f32[3,64,256]{2,1,0:T(8,128)S(1)}, u32[]{:S(2)}, u32[]{:S(2)}) collective-permute-start(f32[3,64,256]{2,1,0:T(8,128)} %get-tuple-element.19), channel_id=1, source_target_pairs={{1,0},{2,1},{3,2},{4,3},{5,4},{6,5},{7,6},{8,7},{9,8},{10,9},{11,1... | collective-permute-start | bytes 589832 | tf_op jit(solution)/shard_map/ppermute | solution.py:266
  23.5 8.4 %collective-permute-start.4 = (f32[3,64,256]{2,1,0:T(8,128)}, f32[3,64,256]{2,1,0:T(8,128)S(1)}, u32[]{:S(2)}, u32[]{:S(2)}) collective-permute-start(f32[3,64,256]{2,1,0:T(8,128)} %get-tuple-element.20), channel_id=1, source_target_pairs={{0,1},{1,2},{2,3},{3,4},{4,5},{5,6},{6,7},{7,8},{8,9},{9,10},{10,1... | collective-permute-start | bytes 589832 | tf_op jit(solution)/shard_map/ppermute | solution.py:265
  25.9 4.6 %collective-permute-start.3 = (f32[8,128]{1,0:T(8,128)S(1)}, f32[8,128]{1,0:T(8,128)S(1)}, u32[]{:S(2)}, u32[]{:S(2)}) collective-permute-start(f32[8,128]{1,0:T(8,128)S(1)} %max.17), channel_id=1, source_target_pairs={{0,8},{1,9},{2,10},{3,11},{4,12},{5,13},{6,14},{7,15},{8,0},{9,1},... | collective-permute-start | bytes 12296 | tf_op jit(solution)/shard_map/ppermute | solution.py:278
  31.9 1.2 %copy-start.2 = (f32[16,64,256]{2,1,0:T(8,128)S(1)}, f32[16,64,256]{2,1,0:T(8,128)}, u32[]{:S(2)}) copy-start(f32[16,64,256]{2,1,0:T(8,128)} %value.5) | copy-start | bytes 3145732
  33.1 1.9 %copy-start.4 = (f32[3,16,64,256]{3,2,1,0:T(8,128)S(1)}, f32[3,16,64,256]{3,2,1,0:T(8,128)}, u32[]{:S(2)}) copy-start(f32[3,16,64,256]{3,2,1,0:T(8,128)} %copy-done.3) | copy-start | bytes 9437188
  35.0 1.9 %copy-start.6 = (f32[3,16,64,256]{3,2,1,0:T(8,128)S(1)}, f32[3,16,64,256]{3,2,1,0:T(8,128)}, u32[]{:S(2)}) copy-start(f32[3,16,64,256]{3,2,1,0:T(8,128)} %copy-done.5) | copy-start | bytes 9437188
  36.9 1.2 %copy-start.8 = (f32[16,64,256]{2,1,0:T(8,128)S(1)}, f32[16,64,256]{2,1,0:T(8,128)}, u32[]{:S(2)}) copy-start(f32[16,64,256]{2,1,0:T(8,128)} %copy-done.7) | copy-start | bytes 3145732
  38.1 1.2 %copy-start.10 = (f32[16,64,256]{2,1,0:T(8,128)S(1)}, f32[16,64,256]{2,1,0:T(8,128)}, u32[]{:S(2)}) copy-start(f32[16,64,256]{2,1,0:T(8,128)} %copy-done.9) | copy-start | bytes 3145732
  51.1 6.1 %collective-permute-start.7 = (f32[3,64,256]{2,1,0:T(8,128)S(1)}, f32[3,64,256]{2,1,0:T(8,128)S(1)}, u32[]{:S(2)}, u32[]{:S(2)}) collective-permute-start(f32[3,64,256]{2,1,0:T(8,128)S(1)} %get-tuple-element.17), channel_id=1, source_target_pairs={{1,0},{2,1},{3,2},{4,3},{5,4},{6,5},{7,6},{8,7},{9,8},{10,9},{11,1... | collective-permute-start | bytes 589832 | tf_op jit(solution)/shard_map/ppermute | solution.py:266
  54.0 7.9 %collective-permute-start.6 = (f32[3,64,256]{2,1,0:T(8,128)S(1)}, f32[3,64,256]{2,1,0:T(8,128)S(1)}, u32[]{:S(2)}, u32[]{:S(2)}) collective-permute-start(f32[3,64,256]{2,1,0:T(8,128)S(1)} %get-tuple-element.18), channel_id=1, source_target_pairs={{0,1},{1,2},{2,3},{3,4},{4,5},{5,6},{6,7},{7,8},{8,9},{9,10},{10,1... | collective-permute-start | bytes 589832 | tf_op jit(solution)/shard_map/ppermute | solution.py:265
  73.6 5.1 %collective-permute-start.9 = (f32[3,64,256]{2,1,0:T(8,128)S(1)}, f32[3,64,256]{2,1,0:T(8,128)S(1)}, u32[]{:S(2)}, u32[]{:S(2)}) collective-permute-start(f32[3,64,256]{2,1,0:T(8,128)S(1)} %get-tuple-element.15), channel_id=1, source_target_pairs={{1,0},{2,1},{3,2},{4,3},{5,4},{6,5},{7,6},{8,7},{9,8},{10,9},{11,1... | collective-permute-start | bytes 589832 | tf_op jit(solution)/shard_map/ppermute | solution.py:266
  75.5 7.9 %collective-permute-start.8 = (f32[3,64,256]{2,1,0:T(8,128)S(1)}, f32[3,64,256]{2,1,0:T(8,128)S(1)}, u32[]{:S(2)}, u32[]{:S(2)}) collective-permute-start(f32[3,64,256]{2,1,0:T(8,128)S(1)} %get-tuple-element.16), channel_id=1, source_target_pairs={{0,1},{1,2},{2,3},{3,4},{4,5},{5,6},{6,7},{7,8},{8,9},{9,10},{10,1... | collective-permute-start | bytes 589832 | tf_op jit(solution)/shard_map/ppermute | solution.py:265

commit v2 on v0

v2 whole, which is shorter than its diff:
```python
import functools

import jax
import jax.numpy as jnp
from jax import lax
from jax.experimental import pallas as pl
from jax.experimental.pallas import tpu as pltpu
from jax.sharding import PartitionSpec as P

LANES = 128
SUB = 8
F32 = jnp.float32
VM = pl.BlockSpec(memory_space=pltpu.VMEM)
SM = pl.BlockSpec(memory_space=pltpu.SMEM)
ANY = pl.BlockSpec(memory_space=pl.ANY)
HBM = pl.BlockSpec(memory_space=pltpu.HBM)
LIMIT = 20 << 20


def rcp(x):
    return pl.reciprocal(x, approx=True)


def twice_square(s):
    return (s + s) * s


def inverse_weights(t, g, left, right):
    base = t * t * (4.0 / 3.0) + 1e-6
    h = base - g
    m = base + g
    l = h + left
    r = h + right
    return rcp(r * r), rcp(l * l), rcp(m * m * (1.0 / 6.0))


def blend(alpha, beta, gamma, far, near):
    gamma = 3.0 * gamma
    return (alpha * far + gamma * near) * rcp(alpha + beta + gamma)


def x_pass(load, cells, span, nz, finish):
    halves = nz // LANES

    def body(i, _):
        y = pl.multiple_of((i // halves) * SUB + span[0], SUB)
        z = pl.multiple_of((i % halves) * LANES, LANES)
        d, s, p, t, q, q2, ir, il, im = ({} for _ in range(9))
        prev = load(0, y, z)
        for r in range(cells + 5):
            nxt = load(r + 1, y, z)
            d[r] = nxt - prev
            prev = nxt
            if r >= 1:
                s[r] = d[r] - d[r - 1]
                p[r] = twice_square(s[r])
            if r >= 2:
                k = r - 1
                t[k] = s[k + 1] - s[k]
                ir[k], il[k], im[k] = inverse_weights(t[k], s[k] * s[k + 1], p[k], p[k + 1])
                if k >= 2:
                    q[k] = t[k] - t[k - 1]
                    q2[k] = q[k] + q[k]
                c = k - 1
                if c >= 3:
                    minus = blend(ir[c - 2], im[c - 1], il[c], q2[c - 1], q[c])
                    plus = blend(il[c + 1], im[c], ir[c - 1], q2[c + 1], q[c])
                    mid = 3.0 * (d[c] + d[c - 1])
                    finish(c - 3, y, z, mid - t[c - 1] - minus, mid - t[c] + plus)
        return 0

    lax.fori_loop(0, (span[1] - span[0]) // SUB * halves, body, 0)


def stage_column(col, work, n):
    wt, wr, wl, wm = work
    for k in range(n // SUB + 1):
        a = 6 + SUB * k
        u0, u1, u2, u3 = (col(a + o) for o in (-1, 0, 1, 2))
        d0, d1, d2 = u1 - u0, u2 - u1, u3 - u2
        s0, s1 = d1 - d0, d2 - d1
        t = s1 - s0
        r, l, m = inverse_weights(t, s0 * s1, twice_square(s0), twice_square(s1))
        wt[a:a + SUB] = t
        wr[a:a + SUB] = r
        wl[a:a + SUB] = l
        wm[a:a + SUB] = m


def column_part(col, work, tile):
    wt, wr, wl, wm = work
    c = SUB + SUB * tile
    at = lambda w, o: w[c + o:c + o + SUB]
    t2, t1, t0, tn = (at(wt, o) for o in (-2, -1, 0, 1))
    q = t0 - t1
    qa = t1 - t2
    qb = tn - t0
    minus = blend(at(wr, -2), at(wm, -1), at(wl, 0), qa + qa, q)
    plus = blend(at(wl, 1), at(wm, 0), at(wr, -1), qb + qb, q)
    mid = 3.0 * (col(c + 1) - col(c - 1))
    return mid - t1 - minus, mid - t0 + plus


def yz_scratch(ny, nz):
    halves = nz // LANES
    return (
        [pltpu.VMEM((2, halves, ny + 2 * SUB, LANES), F32)]
        + [pltpu.VMEM((2, halves, ny + 2 * SUB, LANES), F32)] * 4
        + [pltpu.VMEM((nz + 2 * SUB, LANES), F32)] * 5
        + [pltpu.VMEM((nz, LANES), F32)] * 2
    )


def yz_pass(u, fields, ac, bb, scratch, first, last):
    fp, fm, gain = fields
    yp = scratch[0]
    ywork = scratch[1:5]
    zp = scratch[5]
    zwork = scratch[6:10]
    zm, zd = scratch[10:12]
    _, ny, nz = u.shape
    halves = nz // LANES
    tiles = ny // SUB

    def body(i, _):
        x = first + 2 * i
        for h in range(halves):
            block = u[pl.ds(x, 2), :, h * LANES:(h + 1) * LANES].reshape(2 * ny, LANES)
            zp[SUB + h * LANES:SUB + (h + 1) * LANES] = block.T
        zp[0:SUB] = zp[nz:nz + SUB]
        zp[SUB + nz:2 * SUB + nz] = zp[SUB:2 * SUB]
        for r in range(2):
            for h in range(halves):
                for tile in range(tiles):
                    yp[r, h, SUB + tile * SUB:2 * SUB + tile * SUB] = u[x + r, tile * SUB:(tile + 1) * SUB, h * LANES:(h + 1) * LANES]
                yp[r, h, 0:SUB] = jnp.broadcast_to(u[x + r, 0:1, h * LANES:(h + 1) * LANES], (SUB, LANES))
                yp[r, h, SUB + ny:2 * SUB + ny] = jnp.broadcast_to(u[x + r, ny - 1:ny, h * LANES:(h + 1) * LANES], (SUB, LANES))
        zcol = lambda o: zp[o:o + SUB]
        stage_column(zcol, zwork, nz)
        for tile in range(nz // SUB):
            m, p = column_part(zcol, zwork, tile)
            zm[tile * SUB:(tile + 1) * SUB] = m
            zd[tile * SUB:(tile + 1) * SUB] = p
        for h in range(halves):
            m = zm[h * LANES:(h + 1) * LANES].T
            p = zd[h * LANES:(h + 1) * LANES].T
            for r in range(2):
                ycol = lambda o: yp[r, h, o:o + SUB]
                work = [w.at[r, h] for w in ywork]
                stage_column(ycol, work, ny)
                for tile in range(tiles):
                    ym, yq = column_part(ycol, work, tile)
                    a = r * ny + tile * SUB
                    zmm, zpp = m[a:a + SUB], p[a:a + SUB]
                    at = (x + r, slice(tile * SUB, (tile + 1) * SUB), slice(h * LANES, (h + 1) * LANES))
                    f = lambda w, k: w[(k,) + at]
                    ac[at] = f(fp, 1) * yq + f(fm, 1) * ym + (f(fp, 2) * zpp + f(fm, 2) * zmm)
                    bb[at] = f(gain, 1) * (yq + ym) + f(gain, 2) * (zpp + zmm)
        return 0

    lax.fori_loop(0, (last - first) // 2, body, 0)


def parity():
    return lax.rem(lax.axis_index("gx"), 2)


def first_slab():
    return lax.axis_index("gx") == 0


def last_slab():
    return lax.axis_index("gx") == lax.axis_size("gx") - 1


def call(kernel, ins, outs, scratch, args, us):
    return pl.pallas_call(
        kernel,
        in_specs=ins,
        out_specs=[s for s, _ in outs],
        out_shape=[(pltpu.VMEM(shape, F32) if s is VM else jax.ShapeDtypeStruct(shape, F32)) for s, shape in outs],
        scratch_shapes=scratch,
        cost_estimate=pl.CostEstimate(flops=int(us * 1.15e9), bytes_accessed=0, transcendentals=0),
        compiler_params=pltpu.CompilerParams(vmem_limit_bytes=LIMIT),
    )(*args)


def send_rows(u, odd, near, far):
    last = u.shape[0] - 3

    def body(r, _):
        if near is not None:
            near[r] = u[(1 - odd) * last + r]
        if far is not None:
            far[r] = u[odd * last + r]
        return 0

    lax.fori_loop(0, 3, body, 0)


def prep_kernel(chunk, value, drift, gain, fp, fm, gv, vv, near, top, dv, sems, gsems, vsem):
    rows, ny, nz = value.shape
    n = rows // chunk
    moves = []
    for i in range(n):
        at = pl.ds(i * chunk, chunk)
        a = pltpu.make_async_copy(drift.at[:, at], dv.at[:, at], sems.at[i])
        b = pltpu.make_async_copy(gain.at[:, at], gv.at[:, at], gsems.at[i])
        a.start()
        b.start()
        moves.append((a, b))
    keep = pltpu.make_async_copy(value, vv, vsem.at[0])
    keep.start()
    near[3] = jnp.zeros((ny, nz), F32)
    best = jnp.zeros((SUB, LANES), F32)
    for i in range(n):
        moves[i][0].wait()
        moves[i][1].wait()

        def body(j, best):
            x = i * chunk + j // (ny // SUB)
            y = pl.multiple_of((j % (ny // SUB)) * SUB, SUB)
            for h in range(nz // LANES):
                at = (x, pl.ds(y, SUB), slice(h * LANES, (h + 1) * LANES))
                speed = None
                for k in range(3):
                    a = dv[(k,) + at]
                    w = jnp.abs(a) + jnp.abs(gv[(k,) + at])
                    fp[(k,) + at] = a - w
                    fm[(k,) + at] = a + w
                    speed = w if speed is None else speed + w
                best = jnp.maximum(best, speed)
            return best

        best = lax.fori_loop(0, chunk * (ny // SUB), body, best, unroll=4)
    top[...] = best
    near[3, :SUB, :LANES] = best
    keep.wait()
    send_rows(vv, parity(), near, None)


def merge_kernel(vv, top, near, dep, far, both):
    best = jnp.maximum(top[...], near[3, :SUB, :LANES])
    both[...] = best
    far[3] = jnp.zeros(vv.shape[1:], F32)
    far[3, :SUB, :LANES] = best
    send_rows(vv, parity(), None, far)


def bounds_kernel(dep, target, obstacle, lo, hi, tv, ov, tsems, osems):
    rows, ny, nz = lo.shape
    n = tsems.shape[0]
    chunk = rows // n
    moves = []
    for i in range(n):
        at = pl.ds(i * chunk, chunk)
        a = pltpu.make_async_copy(target.at[at], tv.at[at], tsems.at[i])
        b = pltpu.make_async_copy(obstacle.at[at], ov.at[at], osems.at[i])
        a.start()
        b.start()
        moves.append((a, b))
    for i in range(n):
        moves[i][0].wait()
        moves[i][1].wait()

        def body(x, _):
            lo[x] = jnp.where(ov[x] == 1, 1.0, -jnp.inf)
            hi[x] = jnp.where(tv[x] == 1, -1.0, jnp.inf)
            return 0

        lax.fori_loop(i * chunk, (i + 1) * chunk, body, 0)


def yz_kernel(u, fp, fm, gain, dep, ac, bb, done, *scratch):
    yz_pass(u, (fp, fm, gain), ac, bb, scratch, 0, u.shape[0])
    done[...] = jnp.zeros_like(done)


def x_all(u, near, far, fields, ac, bb, span, finish):
    rows, ny, nz = u.shape
    odd = parity() == 1
    fp, fm, gain = fields

    def load(r, y, z):
        at = (pl.ds(y, SUB), pl.ds(z, LANES))
        if r < 3:
            got = jnp.where(odd, near[(r,) + at], far[(r,) + at])
            return jnp.where(first_slab(), u[(0,) + at], got)
        if r >= rows + 3:
            r -= rows + 3
            got = jnp.where(odd, far[(r,) + at], near[(r,) + at])
            return jnp.where(last_slab(), u[(rows - 1,) + at], got)
        return u[(r - 3,) + at]

    def sums(x, y, z, dm, dp):
        at = (x, pl.ds(y, SUB), pl.ds(z, LANES))
        a = ac[at] + fp[(0,) + at] * dp + fm[(0,) + at] * dm
        b = bb[at] + gain[(0,) + at] * (dp + dm)
        finish(x, y, z, a + jnp.abs(b))

    x_pass(load, rows, span, nz, sums)


def rate_x_kernel(span, u, near, far, fp, fm, gain, ac, bb, dep, total):
    def finish(x, y, z, s):
        total[x, pl.ds(y - span[0], SUB), pl.ds(z, LANES)] = s

    x_all(u, near, far, (fp, fm, gain), ac, bb, span, finish)


def first_kernel(mine, other, value, low, high, lo, hi, u, kappa, near, far):
    best = jnp.maximum(mine[...], other[...])
    best = jnp.max(jnp.max(best, axis=0, keepdims=True), axis=1, keepdims=True)
    k = jnp.broadcast_to(0.5 / best / 12.0, (SUB, LANES))
    kappa[...] = k
    rows, ny, nz = value.shape
    half = ny // 2

    def body(x, _):
        for y in range(0, ny, SUB):
            for z in range(0, nz, LANES):
                at = (x, slice(y, y + SUB), slice(z, z + LANES))
                part, o = (low, y) if y < half else (high, y - half)
                new = value[at] - k * part[x, o:o + SUB, z:z + LANES]
                u[at] = jnp.minimum(jnp.maximum(new, lo[at]), hi[at])
        return 0

    lax.fori_loop(0, rows, body, 0)
    send_rows(u, parity(), near, far)


def updater(weights, kappa, value, u, lo, hi, out):
    keep, take = weights

    def finish(x, y, z, total):
        at = (x, pl.ds(y, SUB), pl.ds(z, LANES))
        new = keep * value[at] + take * u[at] - (take * kappa[...]) * total
        out[at] = jnp.minimum(jnp.maximum(new, lo[at]), hi[at])
    return finish


def second_kernel(weights, u, near, far, kappa, value, fp, fm, gain, lo, hi, ac, bb, out, near_out, far_out):
    _, ny, nz = u.shape
    x_all(u, near, far, (fp, fm, gain), ac, bb, (0, ny), updater(weights, kappa, value, u, lo, hi, out))
    send_rows(out, parity(), near_out, far_out)


def third_kernel(weights, u, near, far, kappa, value, fp, fm, gain, lo, hi, ac, bb, out, keep, sems):
    _, ny, nz = u.shape
    finish = updater(weights, kappa, value, u, lo, hi, keep)
    n = sems.shape[0]
    span = ny // n
    moves = []
    for i in range(n):
        x_all(u, near, far, (fp, fm, gain), ac, bb, (i * span, (i + 1) * span), finish)
        at = pl.ds(i * span, span)
        moves.append(pltpu.make_async_copy(keep.at[:, at], out.at[:, at], sems.at[i]))
        moves[-1].start()
    for m in moves:
        m.wait()


def shards(value, drift, gain, target, obstacle):
    count = lax.axis_size("gx")
    value, drift, gain, target, obstacle = (
        pltpu.with_memory_space_constraint(a, pltpu.HBM) for a in (value, drift, gain, target, obstacle))
    rows, ny, nz = value.shape
    flat, deep, tile = (rows, ny, nz), (3, rows, ny, nz), (SUB, LANES)
    ends, more = (3, ny, nz), (4, ny, nz)
    half = (rows, ny // 2, nz)
    pairs = [(i, i ^ 1) for i in range(count)]

    def links(far):
        out = [(i, (i + 2 * far - 1) % count) for i in range(1, count, 2)]
        return out + [(b, a) for a, b in out]

    def swap(x, perm):
        return lax.ppermute(x, "gx", perm)

    chunk = 2
    dma = pltpu.SemaphoreType.DMA
    fp, fm, gv, vv, near, top = call(
        functools.partial(prep_kernel, chunk),
        [HBM, HBM, HBM],
        [(VM, deep)] * 3 + [(VM, flat), (VM, more), (VM, tile)],
        [pltpu.VMEM(deep, F32)] + [dma((rows // chunk,))] * 2 + [dma((1,))],
        (value, drift, gain), 3)
    fields = (fp, fm, gv)
    work = yz_scratch(ny, nz)
    near = swap(near, pairs)
    lo, hi = call(
        bounds_kernel, [ANY, HBM, HBM], [(VM, flat)] * 2,
        [pltpu.VMEM(flat, jnp.int32)] * 2 + [dma((4,))] * 2, (top, target, obstacle), 1)
    far, top = call(merge_kernel, [VM] * 3 + [ANY], [(VM, more), (VM, tile)], [], (vv, top, near, lo), 0.1)
    far = swap(far, links(1))
    ac, bb, done = call(yz_kernel, [VM] * 4 + [ANY], [(VM, flat)] * 2 + [(VM, tile)], work, (vv,) + fields + (top,), 6)
    top = jnp.maximum(jnp.maximum(top, done), far[3, :SUB, :LANES])
    other = swap(top, pairs)

    def rate_x(span, dep):
        return call(
            functools.partial(rate_x_kernel, span), [VM] * 8 + [ANY], [(VM, half)], [],
            (vv, near, far) + fields + (ac, bb, dep), 1.7)[0]

    low = rate_x((0, ny // 2), top)
    reach = 3
    top = jnp.maximum(top, other)
    dep = top
    while reach < count // 2:
        top = jnp.maximum(top, swap(top, links(reach)))
        other = swap(top, pairs)
        reach *= 3
        if reach < count // 2:
            top = jnp.maximum(top, other)
    high = rate_x((ny // 2, ny), dep)
    u, kappa, near, far = call(
        first_kernel, [VM] * 7, [(VM, flat), (VM, tile), (VM, ends), (VM, ends)], [],
        (top, other, vv, low, high, lo, hi), 1)
    for i, weights in enumerate(((0.75, 0.25), (1 / 3, 2 / 3))):
        far = swap(far, links(1))
        near = swap(near, pairs)
        ac, bb, _ = call(yz_kernel, [VM] * 4 + [ANY], [(VM, flat)] * 2 + [(VM, tile)], work, (u,) + fields + (kappa,), 6)
        args = (u, near, far, kappa, vv) + fields + (lo, hi, ac, bb)
        if i == 0:
            u, near, far = call(
                functools.partial(second_kernel, weights), [VM] * 12,
                [(VM, flat), (VM, ends), (VM, ends)], [], args, 3)
        else:
            return call(
                functools.partial(third_kernel, weights), [VM] * 12,
                [(ANY, flat)], [pltpu.VMEM(flat, F32), dma((4,))], args, 3)[0]


def solution(mesh):
    flat = P(("group", "gx"), None, None)
    deep = P(None, ("group", "gx"), None, None)
    return jax.shard_map(
        shards,
        mesh=mesh,
        in_specs=(flat, deep, deep, flat, flat),
        out_specs=flat,
        check_vma=False,
    )
```

time: 139 us -> 49.3 us (0.35)
  the two profiles are of different devices: /device:TPU:1 before, /device:TPU:0 now
where the time goes in v2:
time: 49.3 us; the launch traced here: 49.1 us
  Pallas kernels  32.7 us (66%)
  starting transfers between devices  12.7 us (26%)
  waiting for transfers between devices  3.69 us (7%)
    pallas_call x11, Pallas kernels, call(): pl.pallas_call(kernel, in_specs=ins, out_specs=[s for s, _ in outs], out_...  32.7 us
    ppermute x9, starting transfers between devices, swap(): return lax.ppermute(x, 'gx', perm)  12.7 us
    ppermute x9, waiting for transfers between devices, swap(): return lax.ppermute(x, 'gx', perm)  3.69 us
  transfers between devices with their start and end apart: 9, of which 2 were waited for; matrix products, arithmetic and copies ran while one was open for 0% of the time, Pallas kernels for 47%

profile of v2, /device:TPU:0, one launch (start us, length us, event | category | flops | bytes accessed | tf_op | source)
XLA Modules:
  0.0 49.1 jit_solution(6531535800959843990)
XLA Ops:
  0.0 3.3 %shard_map.55 = (f32[3,16,64,256]{3,2,1,0:T(8,128)S(1)}, f32[3,16,64,256]{3,2,1,0:T(8,128)S(1)}, f32[3,16,64,256]{3,2,1,0:T(8,128)S(1)}, f32[16,64,256]{2,1,0:T(...) custom-call(f32[16,64,256]{2,1,0:T(8,128)} %value.1, f32[3,16,64,256]{3,2,1,0:T(8,128)} %drift.1, ...), custom_call_target="tpu_custom_call" | custom-call | flops 3449999872 | tf_op jit(solution)/shard_map/pallas_call | solution.py:177
  3.3 0.5 %collective-permute-start = (f32[4,64,256]{2,1,0:T(8,128)S(1)}, f32[4,64,256]{2,1,0:T(8,128)S(1)}, u32[]{:S(2)}, u32[]{:S(2)}) collective-permute-start(f32[4,64,256]{2,1,0:T(8,128)S(1)} %get-tuple-element.31), channel_id=1, source_target_pairs={{0,1},{1,0},{2,3},{3,2},{4,5},{5,4},{6,7},{7,6},{8,9},{9,8},{10,11... | collective-permute-start | bytes 786440 | tf_op jit(solution)/shard_map/ppermute | solution.py:378
  3.8 1.6 %shard_map.56 = (f32[16,64,256]{2,1,0:T(8,128)S(1)}, f32[16,64,256]{2,1,0:T(8,128)S(1)}) custom-call(f32[8,128]{1,0:T(8,128)S(1)} %get-tuple-element.30.dep.top, s32[16,64,256]{2,1,0:T(8,128)} %target.1, s32[16,64,256]{2,1,0:T(8,128)} %obstacle.1), custom_call_target="tpu_custom_call" | custom-call | flops 1150000000 | tf_op jit(solution)/shard_map/pallas_call | solution.py:177
  5.4 0.0 collective-permute-done.near
  5.5 5.7 %collective-permute-start.1 = (f32[4,64,256]{2,1,0:T(8,128)S(1)}, f32[4,64,256]{2,1,0:T(8,128)S(1)}, u32[]{:S(2)}, u32[]{:S(2)}) collective-permute-start(f32[4,64,256]{2,1,0:T(8,128)S(1)} %get-tuple-element.38), channel_id=1, source_target_pairs={{1,2},{3,4},{5,6},{7,8},{9,10},{11,12},{13,14},{15,0},{2,1},{4,3},... | collective-permute-start | bytes 786440 | tf_op jit(solution)/shard_map/ppermute | solution.py:378
  11.2 6.0 %shard_map.58 = (f32[16,64,256]{2,1,0:T(8,128)S(1)}, f32[16,64,256]{2,1,0:T(8,128)S(1)}, f32[8,128]{1,0:T(8,128)S(1)}) custom-call(f32[16,64,256]{2,1,0:T(8,128)S(1)} %get-tuple-element.29.vv.u.value, f32[3,16,64,256]{3,2,1,0:T(8,128)S(1)} %get-tuple-element.34.fp, f32[3,16,64,256]{3,2,1,0:T(8,128)S(1)} %get-tuple-element.35.fm, ...), custom_call_target="tpu_custom_call" | custom-call | flops 6899999744 | tf_op jit(solution)/shard_map/pallas_call | solution.py:177
  17.2 0.0 collective-permute-done.1.far
  17.3 0.1 collective-permute-start.2
  17.3 1.2 %collective-permute-done.2 = f32[8,128]{1,0:T(8,128)S(1)} collective-permute-done((f32[8,128]{1,0:T(8,128)S(1)}, f32[8,128]{1,0:T(8,128)S(1)}, u32[]{:S(2)}, u32[]{:S(2)}) %collective-permute-start.2) | collective-permute-done | bytes 4128 | tf_op jit(solution)/shard_map/ppermute | solution.py:378
  18.5 1.2 %collective-permute-start.3 = (f32[8,128]{1,0:T(8,128)S(1)}, f32[8,128]{1,0:T(8,128)S(1)}, u32[]{:S(2)}, u32[]{:S(2)}) collective-permute-start(f32[8,128]{1,0:T(8,128)S(1)} %max.14.dep), channel_id=1, source_target_pairs={{1,6},{3,8},{5,10},{7,12},{9,14},{11,0},{13,2},{15,4},{6,1},{8,3},... | collective-permute-start | bytes 12296 | tf_op jit(solution)/shard_map/ppermute | solution.py:378
  19.7 1.1 %shard_map.59.low = f32[16,32,256]{2,1,0:T(8,128)S(1)} custom-call(f32[16,64,256]{2,1,0:T(8,128)S(1)} %get-tuple-element.29.vv.u.value, f32[4,64,256]{2,1,0:T(8,128)S(1)} %collective-permute-done.near, f32[4,64,256]{2,1,0:T(8,128)S(1)} %collective-permute-done.1.far, f32[3,16,64,256]{3,2,1,0:T(8,128)S(1)} %get-tuple-element.34.fp, ...), custom_call_target="tpu_custom_call" | custom-call | flops 1955000064 | tf_op jit(solution)/shard_map/pallas_call | solution.py:177
  20.8 2.5 %collective-permute-done.3 = f32[8,128]{1,0:T(8,128)S(1)} collective-permute-done((f32[8,128]{1,0:T(8,128)S(1)}, f32[8,128]{1,0:T(8,128)S(1)}, u32[]{:S(2)}, u32[]{:S(2)}) %collective-permute-start.3) | collective-permute-done | bytes 4128 | tf_op jit(solution)/shard_map/ppermute | solution.py:378
  23.3 0.0 collective-permute-start.4
  23.3 1.1 %shard_map.60.high = f32[16,32,256]{2,1,0:T(8,128)S(1)} custom-call(f32[16,64,256]{2,1,0:T(8,128)S(1)} %get-tuple-element.29.vv.u.value, f32[4,64,256]{2,1,0:T(8,128)S(1)} %collective-permute-done.near, f32[4,64,256]{2,1,0:T(8,128)S(1)} %collective-permute-done.1.far, f32[3,16,64,256]{3,2,1,0:T(8,128)S(1)} %get-tuple-element.34.fp, ...), custom_call_target="tpu_custom_call" | custom-call | flops 1955000064 | tf_op jit(solution)/shard_map/pallas_call | solution.py:177
  24.5 0.0 collective-permute-done.4.other
  24.5 0.4 shard_map.61
  24.9 0.6 %collective-permute-start.5 = (f32[3,64,256]{2,1,0:T(8,128)S(1)}, f32[3,64,256]{2,1,0:T(8,128)S(1)}, u32[]{:S(2)}, u32[]{:S(2)}) collective-permute-start(f32[3,64,256]{2,1,0:T(8,128)S(1)} %get-tuple-element.43), channel_id=1, source_target_pairs={{0,1},{1,0},{2,3},{3,2},{4,5},{5,4},{6,7},{7,6},{8,9},{9,8},{10,11... | collective-permute-start | bytes 589832 | tf_op jit(solution)/shard_map/ppermute | solution.py:378
  25.5 2.4 %collective-permute-start.6 = (f32[3,64,256]{2,1,0:T(8,128)S(1)}, f32[3,64,256]{2,1,0:T(8,128)S(1)}, u32[]{:S(2)}, u32[]{:S(2)}) collective-permute-start(f32[3,64,256]{2,1,0:T(8,128)S(1)} %get-tuple-element.44), channel_id=1, source_target_pairs={{1,2},{3,4},{5,6},{7,8},{9,10},{11,12},{13,14},{15,0},{2,1},{4,3},... | collective-permute-start | bytes 589832 | tf_op jit(solution)/shard_map/ppermute | solution.py:378
  27.9 6.6 %shard_map.62 = (f32[16,64,256]{2,1,0:T(8,128)S(1)}, f32[16,64,256]{2,1,0:T(8,128)S(1)}, f32[8,128]{1,0:T(8,128)}) custom-call(f32[16,64,256]{2,1,0:T(8,128)S(1)} %get-tuple-element.42.u, f32[3,16,64,256]{3,2,1,0:T(8,128)S(1)} %get-tuple-element.34.fp, f32[3,16,64,256]{3,2,1,0:T(8,128)S(1)} %get-tuple-element.35.fm, ...), custom_call_target="tpu_custom_call" | custom-call | flops 6899999744 | tf_op jit(solution)/shard_map/pallas_call | solution.py:177
  34.5 0.0 collective-permute-done.5.near
  34.5 0.0 collective-permute-done.6.far
  34.5 2.6 %shard_map.63 = (f32[16,64,256]{2,1,0:T(8,128)S(1)}, f32[3,64,256]{2,1,0:T(8,128)S(1)}, f32[3,64,256]{2,1,0:T(8,128)S(1)}) custom-call(f32[16,64,256]{2,1,0:T(8,128)S(1)} %get-tuple-element.42.u, f32[3,64,256]{2,1,0:T(8,128)S(1)} %collective-permute-done.5.near, f32[3,64,256]{2,1,0:T(8,128)S(1)} %collective-permute-done.6.far, ...), custom_call_target="tpu_custom_call" | custom-call | flops 3449999872 | tf_op jit(solution)/shard_map/pallas_call | solution.py:177
  37.1 0.1 collective-permute-start.7
  37.2 2.1 %collective-permute-start.8 = (f32[3,64,256]{2,1,0:T(8,128)S(1)}, f32[3,64,256]{2,1,0:T(8,128)S(1)}, u32[]{:S(2)}, u32[]{:S(2)}) collective-permute-start(f32[3,64,256]{2,1,0:T(8,128)S(1)} %get-tuple-element.50), channel_id=1, source_target_pairs={{1,2},{3,4},{5,6},{7,8},{9,10},{11,12},{13,14},{15,0},{2,1},{4,3},... | collective-permute-start | bytes 589832 | tf_op jit(solution)/shard_map/ppermute | solution.py:378
  39.3 6.5 %shard_map.64 = (f32[16,64,256]{2,1,0:T(8,128)S(1)}, f32[16,64,256]{2,1,0:T(8,128)S(1)}, f32[8,128]{1,0:T(8,128)}) custom-call(f32[16,64,256]{2,1,0:T(8,128)S(1)} %get-tuple-element.48.u, f32[3,16,64,256]{3,2,1,0:T(8,128)S(1)} %get-tuple-element.34.fp, f32[3,16,64,256]{3,2,1,0:T(8,128)S(1)} %get-tuple-element.35.fm, ...), custom_call_target="tpu_custom_call" | custom-call | flops 6899999744 | tf_op jit(solution)/shard_map/pallas_call | solution.py:177
  45.8 0.0 collective-permute-done.7.near
  45.8 0.0 collective-permute-done.8.far
  45.8 3.3 %shard_map.65 = f32[16,64,256]{2,1,0:T(8,128)} custom-call(f32[16,64,256]{2,1,0:T(8,128)S(1)} %get-tuple-element.48.u, f32[3,64,256]{2,1,0:T(8,128)S(1)} %collective-permute-done.7.near, f32[3,64,256]{2,1,0:T(8,128)S(1)} %collective-permute-done.8.far, f32[8,128]{1,0:T(8,128)S(1)} %get-tuple-element.45.dep.kappa, ...), custom_call_target="tpu_custom_call" | custom-call | flops 3449999872 | tf_op jit(solution)/shard_map/pallas_call | solution.py:177
  (4 shorter events, 0.0 us)
Async XLA Ops:
  3.3 2.2 %collective-permute-start = (f32[4,64,256]{2,1,0:T(8,128)S(1)}, f32[4,64,256]{2,1,0:T(8,128)S(1)}, u32[]{:S(2)}, u32[]{:S(2)}) collective-permute-start(f32[4,64,256]{2,1,0:T(8,128)S(1)} %get-tuple-element.31), channel_id=1, source_target_pairs={{0,1},{1,0},{2,3},{3,2},{4,5},{5,4},{6,7},{7,6},{8,9},{9,8},{10,11... | collective-permute-start | bytes 786440 | tf_op jit(solution)/shard_map/ppermute | solution.py:378
  5.5 11.7 %collective-permute-start.1 = (f32[4,64,256]{2,1,0:T(8,128)S(1)}, f32[4,64,256]{2,1,0:T(8,128)S(1)}, u32[]{:S(2)}, u32[]{:S(2)}) collective-permute-start(f32[4,64,256]{2,1,0:T(8,128)S(1)} %get-tuple-element.38), channel_id=1, source_target_pairs={{1,2},{3,4},{5,6},{7,8},{9,10},{11,12},{13,14},{15,0},{2,1},{4,3},... | collective-permute-start | bytes 786440 | tf_op jit(solution)/shard_map/ppermute | solution.py:378
  17.3 1.2 %collective-permute-start.2 = (f32[8,128]{1,0:T(8,128)S(1)}, f32[8,128]{1,0:T(8,128)S(1)}, u32[]{:S(2)}, u32[]{:S(2)}) collective-permute-start(f32[8,128]{1,0:T(8,128)S(1)} %fusion.dep), channel_id=1, source_target_pairs={{0,1},{1,0},{2,3},{3,2},{4,5},{5,4},{6,7},{7,6},{8,9},{9,8},{10,11... | collective-permute-start | bytes 12296 | tf_op jit(solution)/shard_map/ppermute | solution.py:378
  18.5 4.8 %collective-permute-start.3 = (f32[8,128]{1,0:T(8,128)S(1)}, f32[8,128]{1,0:T(8,128)S(1)}, u32[]{:S(2)}, u32[]{:S(2)}) collective-permute-start(f32[8,128]{1,0:T(8,128)S(1)} %max.14.dep), channel_id=1, source_target_pairs={{1,6},{3,8},{5,10},{7,12},{9,14},{11,0},{13,2},{15,4},{6,1},{8,3},... | collective-permute-start | bytes 12296 | tf_op jit(solution)/shard_map/ppermute | solution.py:378
  23.3 1.2 %collective-permute-start.4 = (f32[8,128]{1,0:T(8,128)S(1)}, f32[8,128]{1,0:T(8,128)S(1)}, u32[]{:S(2)}, u32[]{:S(2)}) collective-permute-start(f32[8,128]{1,0:T(8,128)S(1)} %max.15.mine), channel_id=1, source_target_pairs={{0,1},{1,0},{2,3},{3,2},{4,5},{5,4},{6,7},{7,6},{8,9},{9,8},{10,11... | collective-permute-start | bytes 12296 | tf_op jit(solution)/shard_map/ppermute | solution.py:378
  24.9 9.6 %collective-permute-start.5 = (f32[3,64,256]{2,1,0:T(8,128)S(1)}, f32[3,64,256]{2,1,0:T(8,128)S(1)}, u32[]{:S(2)}, u32[]{:S(2)}) collective-permute-start(f32[3,64,256]{2,1,0:T(8,128)S(1)} %get-tuple-element.43), channel_id=1, source_target_pairs={{0,1},{1,0},{2,3},{3,2},{4,5},{5,4},{6,7},{7,6},{8,9},{9,8},{10,11... | collective-permute-start | bytes 589832 | tf_op jit(solution)/shard_map/ppermute | solution.py:378
  25.5 9.0 %collective-permute-start.6 = (f32[3,64,256]{2,1,0:T(8,128)S(1)}, f32[3,64,256]{2,1,0:T(8,128)S(1)}, u32[]{:S(2)}, u32[]{:S(2)}) collective-permute-start(f32[3,64,256]{2,1,0:T(8,128)S(1)} %get-tuple-element.44), channel_id=1, source_target_pairs={{1,2},{3,4},{5,6},{7,8},{9,10},{11,12},{13,14},{15,0},{2,1},{4,3},... | collective-permute-start | bytes 589832 | tf_op jit(solution)/shard_map/ppermute | solution.py:378
  37.1 8.7 %collective-permute-start.7 = (f32[3,64,256]{2,1,0:T(8,128)S(1)}, f32[3,64,256]{2,1,0:T(8,128)S(1)}, u32[]{:S(2)}, u32[]{:S(2)}) collective-permute-start(f32[3,64,256]{2,1,0:T(8,128)S(1)} %get-tuple-element.49), channel_id=1, source_target_pairs={{0,1},{1,0},{2,3},{3,2},{4,5},{5,4},{6,7},{7,6},{8,9},{9,8},{10,11... | collective-permute-start | bytes 589832 | tf_op jit(solution)/shard_map/ppermute | solution.py:378
  37.2 8.6 %collective-permute-start.8 = (f32[3,64,256]{2,1,0:T(8,128)S(1)}, f32[3,64,256]{2,1,0:T(8,128)S(1)}, u32[]{:S(2)}, u32[]{:S(2)}) collective-permute-start(f32[3,64,256]{2,1,0:T(8,128)S(1)} %get-tuple-element.50), channel_id=1, source_target_pairs={{1,2},{3,4},{5,6},{7,8},{9,10},{11,12},{13,14},{15,0},{2,1},{4,3},... | collective-permute-start | bytes 589832 | tf_op jit(solution)/shard_map/ppermute | solution.py:378

commit v3 on v2

v3 whole, which is shorter than its diff:
```python
import functools

import jax
import jax.numpy as jnp
from jax import lax
from jax.experimental import pallas as pl
from jax.experimental.pallas import tpu as pltpu
from jax.sharding import PartitionSpec as P

LANES = 128
SUB = 8
F32 = jnp.float32
VM = pl.BlockSpec(memory_space=pltpu.VMEM)
SM = pl.BlockSpec(memory_space=pltpu.SMEM)
ANY = pl.BlockSpec(memory_space=pl.ANY)
HBM = pl.BlockSpec(memory_space=pltpu.HBM)
LIMIT = 20 << 20


def rcp(x):
    return pl.reciprocal(x, approx=True)


def twice_square(s):
    return (s + s) * s


def inverse_weights(t, g, left, right):
    base = t * t * (4.0 / 3.0) + 1e-6
    h = base - g
    m = base + g
    l = h + left
    r = h + right
    return rcp(r * r), rcp(l * l), rcp(m * m * (1.0 / 6.0))


def blend(alpha, beta, gamma, far, near):
    gamma = 3.0 * gamma
    return (alpha * far + gamma * near) * rcp(alpha + beta + gamma)


def x_pass(load, cells, span, nz, finish, after=None):
    def column(y, z):
        d, s, p, t, q, q2, ir, il, im = ({} for _ in range(9))
        prev = load(0, y, z)
        for r in range(cells + 5):
            nxt = load(r + 1, y, z)
            d[r] = nxt - prev
            prev = nxt
            if r >= 1:
                s[r] = d[r] - d[r - 1]
                p[r] = twice_square(s[r])
            if r >= 2:
                k = r - 1
                t[k] = s[k + 1] - s[k]
                ir[k], il[k], im[k] = inverse_weights(t[k], s[k] * s[k + 1], p[k], p[k + 1])
                if k >= 2:
                    q[k] = t[k] - t[k - 1]
                    q2[k] = q[k] + q[k]
                c = k - 1
                if c >= 3:
                    minus = blend(ir[c - 2], im[c - 1], il[c], q2[c - 1], q[c])
                    plus = blend(il[c + 1], im[c], ir[c - 1], q2[c + 1], q[c])
                    mid = 3.0 * (d[c] + d[c - 1])
                    finish(c - 3, y, z, mid - t[c - 1] - minus, mid - t[c] + plus)

    def body(i, _):
        y = pl.multiple_of(i * SUB + span[0], SUB)
        for z in range(0, nz, LANES):
            column(y, z)
        if after is not None:
            after(i, y)
        return 0

    lax.fori_loop(0, (span[1] - span[0]) // SUB, body, 0)


ORIGIN = SUB + 2
PAD = 3 * SUB


def column_weights(col, work, n):
    wt, wr, wl, wm = work
    for k in range(n // SUB + 1):
        a = SUB + SUB * k
        u0, u1, u2, u3 = (col(a + o) for o in (-1, 0, 1, 2))
        d0, d1, d2 = u1 - u0, u2 - u1, u3 - u2
        s0, s1 = d1 - d0, d2 - d1
        t = s1 - s0
        wt[a:a + SUB] = t
        r, l, m = inverse_weights(t, s0 * s1, twice_square(s0), twice_square(s1))
        wr[a:a + SUB] = r
        wl[a:a + SUB] = l
        wm[a:a + SUB] = m


def column_part(col, work, tile):
    wt, wr, wl, wm = work
    c = ORIGIN + SUB * tile
    at = lambda w, o: w[c + o:c + o + SUB]
    t2, t1, t0, tn = (at(wt, o) for o in (-2, -1, 0, 1))
    q = t0 - t1
    qa = t1 - t2
    qb = tn - t0
    minus = blend(at(wr, -2), at(wm, -1), at(wl, 0), qa + qa, q)
    plus = blend(at(wl, 1), at(wm, 0), at(wr, -1), qb + qb, q)
    mid = 3.0 * (col(c + 1) - col(c - 1))
    return mid - t1 - minus, mid - t0 + plus


def yz_scratch(ny, nz):
    halves = nz // LANES
    vmem = lambda *shape: pltpu.VMEM(shape, F32)
    slot = [vmem(nz + PAD, LANES)] + [vmem(nz, LANES)] * 2 + [vmem(2, halves, ny, LANES)] * 2 + [vmem(halves, 2 * ny, LANES)] * 2
    return (
        [vmem(2, halves, ny + PAD, LANES)] * 5
        + [vmem(nz + PAD, LANES)] * 4
        + slot * 2
    )


def yz_pass(u, fields, ac, bb, scratch, first, last):
    fp, fm, gain = fields
    yp, ywork, zwork = scratch[0], scratch[1:5], scratch[5:9]
    slots = (scratch[9:16], scratch[16:23])
    _, ny, nz = u.shape
    halves = nz // LANES
    tiles = ny // SUB
    pairs = (last - first) // 2

    def forward(i, slot):
        zp = slot[0]
        for h in range(halves):
            block = u[pl.ds(first + 2 * i, 2), :, h * LANES:(h + 1) * LANES].reshape(2 * ny, LANES)
            zp[ORIGIN + h * LANES:ORIGIN + (h + 1) * LANES] = block.T
        zp[ORIGIN - SUB:ORIGIN] = zp[nz + ORIGIN - SUB:nz + ORIGIN]
        zp[ORIGIN + nz:ORIGIN + nz + SUB] = zp[ORIGIN:ORIGIN + SUB]
        zp[PAD - SUB + nz:PAD + nz] = zp[PAD - SUB:PAD]

    def work(i, slot):
        zp, zm, zd, ya, yb, _, _ = slot
        x = first + 2 * i
        zcol = lambda o: zp[o:o + SUB]
        column_weights(zcol, zwork, nz)
        for tile in range(nz // SUB):
            m, p = column_part(zcol, zwork, tile)
            zm[tile * SUB:(tile + 1) * SUB] = m
            zd[tile * SUB:(tile + 1) * SUB] = p
        for r in range(2):
            for h in range(halves):
                z = slice(h * LANES, (h + 1) * LANES)
                for tile in range(tiles):
                    o = ORIGIN + tile * SUB
                    yp[r, h, o:o + SUB] = u[x + r, tile * SUB:(tile + 1) * SUB, z]
                yp[r, h, ORIGIN - SUB:ORIGIN] = jnp.broadcast_to(u[x + r, 0:1, z], (SUB, LANES))
                top = jnp.broadcast_to(u[x + r, ny - 1:ny, z], (SUB, LANES))
                yp[r, h, ORIGIN + ny:ORIGIN + ny + SUB] = top
                yp[r, h, PAD - SUB + ny:PAD + ny] = top
                ycol = lambda o: yp[r, h, o:o + SUB]
                here = [w.at[r, h] for w in ywork]
                column_weights(ycol, here, ny)
                for tile in range(tiles):
                    m, p = column_part(ycol, here, tile)
                    at = (1, x + r, slice(tile * SUB, (tile + 1) * SUB), z)
                    to = (r, h, slice(tile * SUB, (tile + 1) * SUB))
                    ya[to] = fp[at] * p + fm[at] * m
                    yb[to] = gain[at] * (p + m)

    def back(slot):
        _, zm, zd, _, _, tm, td = slot
        for h in range(halves):
            tm[h] = zm[h * LANES:(h + 1) * LANES].T
            td[h] = zd[h * LANES:(h + 1) * LANES].T

    def total(i, slot):
        _, _, _, ya, yb, tm, td = slot
        x = 2 * i
        for h in range(halves):
            for r in range(2):
                for tile in range(tiles):
                    o = r * ny + tile * SUB
                    m, p = tm[h, o:o + SUB], td[h, o:o + SUB]
                    at = (x + r, slice(tile * SUB, (tile + 1) * SUB), slice(h * LANES, (h + 1) * LANES))
                    of = (2, first + x + r) + at[1:]
                    to = (r, h, slice(tile * SUB, (tile + 1) * SUB))
                    ac[at] = ya[to] + (fp[of] * p + fm[of] * m)
                    bb[at] = yb[to] + gain[of] * (p + m)

    forward(0, slots[0])

    def body(j, _):
        forward(2 * j + 1, slots[1])
        work(2 * j, slots[0])
        back(slots[0])
        total(2 * j, slots[0])
        forward(jnp.minimum(2 * j + 2, pairs - 1), slots[0])
        work(2 * j + 1, slots[1])
        back(slots[1])
        total(2 * j + 1, slots[1])
        return 0

    lax.fori_loop(0, pairs // 2, body, 0)


def parity():
    return lax.rem(lax.axis_index("gx"), 2)


def first_slab():
    return lax.axis_index("gx") == 0


def last_slab():
    return lax.axis_index("gx") == lax.axis_size("gx") - 1


def call(kernel, ins, outs, scratch, args, us):
    return pl.pallas_call(
        kernel,
        in_specs=ins,
        out_specs=[s for s, _ in outs],
        out_shape=[(pltpu.VMEM(shape, F32) if s is VM else jax.ShapeDtypeStruct(shape, F32)) for s, shape in outs],
        scratch_shapes=scratch,
        cost_estimate=pl.CostEstimate(flops=int(us * 1.15e9), bytes_accessed=0, transcendentals=0),
        compiler_params=pltpu.CompilerParams(vmem_limit_bytes=LIMIT),
    )(*args)


def send_rows(u, odd, near, far):
    last = u.shape[0] - 3

    def body(r, _):
        near[r] = u[(1 - odd) * last + r]
        far[r] = u[odd * last + r]
        return 0

    lax.fori_loop(0, 3, body, 0)


def prep_kernel(chunk, value, drift, gain, fp, fm, gv, vv, near, far, top, dv, sems, gsems, vsem):
    rows, ny, nz = value.shape
    n = rows // chunk
    moves = []
    for i in range(n):
        at = pl.ds(i * chunk, chunk)
        a = pltpu.make_async_copy(drift.at[:, at], dv.at[:, at], sems.at[i])
        b = pltpu.make_async_copy(gain.at[:, at], gv.at[:, at], gsems.at[i])
        a.start()
        b.start()
        moves.append((a, b))
    keep = pltpu.make_async_copy(value, vv, vsem.at[0])
    keep.start()
    best = jnp.zeros((SUB, LANES), F32)
    for i in range(n):
        moves[i][0].wait()
        moves[i][1].wait()

        def body(j, best):
            x = i * chunk + j // (ny // SUB)
            y = pl.multiple_of((j % (ny // SUB)) * SUB, SUB)
            for h in range(nz // LANES):
                at = (x, pl.ds(y, SUB), slice(h * LANES, (h + 1) * LANES))
                speed = None
                for k in range(3):
                    a = dv[(k,) + at]
                    w = jnp.abs(a) + jnp.abs(gv[(k,) + at])
                    fp[(k,) + at] = a - w
                    fm[(k,) + at] = a + w
                    speed = w if speed is None else speed + w
                best = jnp.maximum(best, speed)
            return best

        best = lax.fori_loop(0, chunk * (ny // SUB), body, best, unroll=4)
    top[...] = best
    keep.wait()
    send_rows(vv, parity(), near, far)


def yz_bounds_kernel(first, last, u, fp, fm, gain, dep, target, obstacle, ac, bb, done, lo, hi, tv, ov, sems, *scratch):
    a = pltpu.make_async_copy(target, tv, sems.at[0])
    b = pltpu.make_async_copy(obstacle, ov, sems.at[1])
    a.start()
    b.start()
    yz_pass(u, (fp, fm, gain), ac, bb, scratch, first, last)
    done[...] = jnp.zeros_like(done)
    a.wait()
    b.wait()

    def body(x, _):
        lo[x] = jnp.where(ov[x] == 1, 1.0, -jnp.inf)
        hi[x] = jnp.where(tv[x] == 1, -1.0, jnp.inf)
        return 0

    lax.fori_loop(0, u.shape[0], body, 0)


def yz_kernel(first, last, u, fp, fm, gain, dep, ac, bb, done, *scratch):
    yz_pass(u, (fp, fm, gain), ac, bb, scratch, first, last)
    done[...] = jnp.zeros_like(done)


def x_all(u, near, far, fields, ac, bb, span, finish, after=None):
    rows, ny, nz = u.shape
    odd = parity() == 1
    fp, fm, gain = fields

    def load(r, y, z):
        at = (pl.ds(y, SUB), pl.ds(z, LANES))
        if r < 3:
            got = jnp.where(odd, near[(r,) + at], far[(r,) + at])
            return jnp.where(first_slab(), u[(0,) + at], got)
        if r >= rows + 3:
            r -= rows + 3
            got = jnp.where(odd, far[(r,) + at], near[(r,) + at])
            return jnp.where(last_slab(), u[(rows - 1,) + at], got)
        return u[(r - 3,) + at]

    size = ac[0].shape[0]

    def part(parts, x, at):
        return parts[0][(x,) + at] if x < size else parts[1][(x - size,) + at]

    def sums(x, y, z, dm, dp):
        at = (x, pl.ds(y, SUB), pl.ds(z, LANES))
        a = part(ac, x, at[1:]) + fp[(0,) + at] * dp + fm[(0,) + at] * dm
        b = part(bb, x, at[1:]) + gain[(0,) + at] * (dp + dm)
        finish(x, y, z, a + jnp.abs(b))

    x_pass(load, rows, span, nz, sums, after)


def rate_x_kernel(u, near, far, fp, fm, gain, ac0, bb0, ac1, bb1, dep, total, done):
    done[...] = jnp.zeros_like(done)

    def finish(x, y, z, s):
        total[x, pl.ds(y, SUB), pl.ds(z, LANES)] = s

    x_all(u, near, far, (fp, fm, gain), (ac0, ac1), (bb0, bb1), (0, u.shape[1]), finish)


def first_kernel(mine, other, value, total, lo, hi, u, kappa, near, far):
    best = jnp.maximum(mine[...], other[...])
    best = jnp.max(jnp.max(best, axis=0, keepdims=True), axis=1, keepdims=True)
    k = jnp.broadcast_to(0.5 / best / 12.0, (SUB, LANES))
    kappa[...] = k
    rows, ny, nz = value.shape

    def body(x, _):
        for y in range(0, ny, SUB):
            for z in range(0, nz, LANES):
                at = (x, slice(y, y + SUB), slice(z, z + LANES))
                new = value[at] - k * total[at]
                u[at] = jnp.minimum(jnp.maximum(new, lo[at]), hi[at])
        return 0

    lax.fori_loop(0, rows, body, 0)
    send_rows(u, parity(), near, far)


def updater(weights, kappa, value, u, lo, hi, out):
    keep, take = weights

    def finish(x, y, z, total):
        at = (x, pl.ds(y, SUB), pl.ds(z, LANES))
        new = keep * value[at] + take * u[at] - (take * kappa[...]) * total
        out[at] = jnp.minimum(jnp.maximum(new, lo[at]), hi[at])
    return finish


def second_kernel(weights, u, near, far, kappa, value, fp, fm, gain, lo, hi, ac, bb, out, near_out, far_out):
    _, ny, nz = u.shape
    x_all(u, near, far, (fp, fm, gain), (ac,), (bb,), (0, ny), updater(weights, kappa, value, u, lo, hi, out))
    send_rows(out, parity(), near_out, far_out)


def third_kernel(weights, u, near, far, kappa, value, fp, fm, gain, lo, hi, ac, bb, out, keep, sems):
    _, ny, nz = u.shape

    def move(i, y):
        at = pl.ds(y, SUB)
        return pltpu.make_async_copy(keep.at[:, at], out.at[:, at], sems.at[i])

    x_all(u, near, far, (fp, fm, gain), (ac,), (bb,), (0, ny), updater(weights, kappa, value, u, lo, hi, keep),
          lambda i, y: move(i, y).start())

    def wait(i, _):
        move(i, pl.multiple_of(i * SUB, SUB)).wait()
        return 0

    lax.fori_loop(0, ny // SUB, wait, 0)


def shards(value, drift, gain, target, obstacle):
    count = lax.axis_size("gx")
    value, drift, gain, target, obstacle = (
        pltpu.with_memory_space_constraint(a, pltpu.HBM) for a in (value, drift, gain, target, obstacle))
    rows, ny, nz = value.shape
    flat, deep, tile = (rows, ny, nz), (3, rows, ny, nz), (SUB, LANES)
    ends = (3, ny, nz)
    pairs = [(i, i ^ 1) for i in range(count)]

    links = [(i, (i + 1) % count) for i in range(1, count, 2)]
    links += [(b, a) for a, b in links]
    chips = count // 2
    order = list(range(0, chips, 2)) + list(range(chips - 1 - chips % 2, 0, -2))

    def ring(reach):
        out = [(2 * order[i] + 1, 2 * order[(i + reach) % chips]) for i in range(chips)]
        return out + [(b, a) for a, b in out]

    def swap(x, perm):
        return lax.ppermute(x, "gx", perm)

    chunk = 2
    dma = pltpu.SemaphoreType.DMA
    fp, fm, gv, vv, near, far, top = call(
        functools.partial(prep_kernel, chunk),
        [HBM, HBM, HBM],
        [(VM, deep)] * 3 + [(VM, flat), (VM, ends), (VM, ends), (VM, tile)],
        [pltpu.VMEM(deep, F32)] + [dma((rows // chunk,))] * 2 + [dma((1,))],
        (value, drift, gain), 3)
    fields = (fp, fm, gv)
    work = yz_scratch(ny, nz)
    other = swap(top, pairs)
    far = swap(far, links)
    near = swap(near, pairs)

    def join(top, other, done):
        return jnp.maximum(jnp.maximum(top, other), done)

    def rate_yz(u, first, last, dep, us):
        part = (last - first, ny, nz)
        return call(functools.partial(yz_kernel, first, last), [VM] * 4 + [ANY],
                    [(VM, part)] * 2 + [(VM, tile)], work, (u,) + fields + (dep,), us)

    mid = 2 * (3 * rows // 8)
    top = jnp.maximum(top, other)
    other = swap(top, ring(1))
    ac0, bb0, done = rate_yz(vv, 0, mid, top, 4)
    top = join(top, other, done)
    other = swap(top, pairs)
    ac1, bb1, done, lo, hi = call(
        functools.partial(yz_bounds_kernel, mid, rows), [VM] * 4 + [ANY, HBM, HBM],
        [(VM, (rows - mid, ny, nz))] * 2 + [(VM, tile)] + [(VM, flat)] * 2,
        [pltpu.VMEM(flat, jnp.int32)] * 2 + [dma((2,))] + work, (vv,) + fields + (top, target, obstacle), 3)
    top = join(top, other, done)
    reach = 3
    other = swap(top, ring(reach))
    total, done = call(
        rate_x_kernel, [VM] * 10 + [ANY], [(VM, flat), (VM, tile)], [],
        (vv, near, far) + fields + (ac0, bb0, ac1, bb1, top), 2.4)
    top = join(top, other, done)
    other = swap(top, pairs)
    while 3 * reach < count // 2:
        reach *= 3
        top = jnp.maximum(top, other)
        top = jnp.maximum(top, swap(top, ring(reach)))
        other = swap(top, pairs)
    u, kappa, near, far = call(
        first_kernel, [VM] * 6, [(VM, flat), (VM, tile), (VM, ends), (VM, ends)], [],
        (top, other, vv, total, lo, hi), 1)
    for i, weights in enumerate(((0.75, 0.25), (1 / 3, 2 / 3))):
        far = swap(far, links)
        near = swap(near, pairs)
        ac, bb, _ = rate_yz(u, 0, rows, kappa, 6)
        args = (u, near, far, kappa, vv) + fields + (lo, hi, ac, bb)
        if i == 0:
            u, near, far = call(
                functools.partial(second_kernel, weights), [VM] * 12,
                [(VM, flat), (VM, ends), (VM, ends)], [], args, 3)
        else:
            return call(
                functools.partial(third_kernel, weights), [VM] * 12,
                [(ANY, flat)], [pltpu.VMEM(flat, F32), dma((ny // SUB,))], args, 3)[0]


def solution(mesh):
    flat = P(("group", "gx"), None, None)
    deep = P(None, ("group", "gx"), None, None)
    return jax.shard_map(
        shards,
        mesh=mesh,
        in_specs=(flat, deep, deep, flat, flat),
        out_specs=flat,
        check_vma=False,
    )
```

time: 49.3 us -> 44.6 us (0.905)
  Pallas kernels: 32.7 us -> 28.8 us
  waiting for transfers between devices: 3.69 us -> 2.2 us
  starting transfers between devices: 12.7 us -> 13.3 us
    pallas_call x11 -> x9, Pallas kernels: 32.7 us -> 28.8 us  [call(): pl.pallas_call(kernel, in_specs=ins, out_specs=[s for s, _ in outs], out_...]
    ppermute x9 -> x11, waiting for transfers between devices: 3.69 us -> 2.2 us  [swap(): return lax.ppermute(x, 'gx', perm)]
    ppermute x9 -> x11, starting transfers between devices: 12.7 us -> 13.3 us  [swap(): return lax.ppermute(x, 'gx', perm)]
  transfers between devices with their start and end apart: 9 -> 11, of which waited for: 2 -> 2; matrix products, arithmetic and copies ran while one was open for 0% -> 0% of each run, Pallas kernels for 47% -> 44%
where the time goes in v3:
time: 44.6 us; the launch traced here: 44.4 us
  Pallas kernels  28.8 us (65%)
  starting transfers between devices  13.3 us (30%)
  waiting for transfers between devices  2.2 us (5%)
    pallas_call x9, Pallas kernels, call(): pl.pallas_call(kernel, in_specs=ins, out_specs=[s for s, _ in outs], out_...  28.8 us
    ppermute x11, starting transfers between devices, swap(): return lax.ppermute(x, 'gx', perm)  13.3 us
    ppermute x11, waiting for transfers between devices, swap(): return lax.ppermute(x, 'gx', perm)  2.2 us
  transfers between devices with their start and end apart: 11, of which 2 were waited for; matrix products, arithmetic and copies ran while one was open for 0% of the time, Pallas kernels for 44%

profile of v3, /device:TPU:0, one launch (start us, length us, event | category | flops | bytes accessed | tf_op | source)
XLA Modules:
  0.0 44.4 jit_solution(13390488402912201132)
XLA Ops:
  0.0 3.3 %shard_map.55 = (f32[3,16,64,256]{3,2,1,0:T(8,128)S(1)}, f32[3,16,64,256]{3,2,1,0:T(8,128)S(1)}, f32[3,16,64,256]{3,2,1,0:T(8,128)S(1)}, f32[16,64,256]{2,1,0:T(...) custom-call(f32[16,64,256]{2,1,0:T(8,128)} %value.1, ...), custom_call_target="tpu_custom_call" | custom-call | flops 3449999872 | tf_op jit(solution)/shard_map/pallas_call | solution.py:218
  3.3 0.5 %collective-permute-start = (f32[8,128]{1,0:T(8,128)S(1)}, f32[8,128]{1,0:T(8,128)S(1)}, u32[]{:S(2)}, u32[]{:S(2)}) collective-permute-start(f32[8,128]{1,0:T(8,128)S(1)} %get-tuple-element.33), channel_id=1, source_target_pairs={{0,1},{1,0},{2,3},{3,2},{4,5},{5,4},{6,7},{7,6},{8,9},{9,8},{10,11... | collective-permute-start | bytes 12296 | tf_op jit(solution)/shard_map/ppermute | solution.py:412
  3.8 0.1 collective-permute-start.4
  3.9 5.7 %collective-permute-start.5 = (f32[3,64,256]{2,1,0:T(8,128)S(1)}, f32[3,64,256]{2,1,0:T(8,128)S(1)}, u32[]{:S(2)}, u32[]{:S(2)}) collective-permute-start(f32[3,64,256]{2,1,0:T(8,128)S(1)} %get-tuple-element.41), channel_id=1, source_target_pairs={{1,2},{3,4},{5,6},{7,8},{9,10},{11,12},{13,14},{15,0},{2,1},{4,3},... | collective-permute-start | bytes 589832 | tf_op jit(solution)/shard_map/ppermute | solution.py:412
  9.6 0.0 collective-permute-done
  9.6 0.0 collective-permute-start.1
  9.6 4.0 %shard_map.56 = (f32[12,64,256]{2,1,0:T(8,128)S(1)}, f32[12,64,256]{2,1,0:T(8,128)S(1)}, f32[8,128]{1,0:T(8,128)S(1)}) custom-call(f32[16,64,256]{2,1,0:T(8,128)S(1)} %get-tuple-element.34.u.value, f32[3,16,64,256]{3,2,1,0:T(8,128)S(1)} %get-tuple-element.35.fp, f32[3,16,64,256]{3,2,1,0:T(8,128)S(1)} %get-tuple-element.36.fm, ...), custom_call_target="tpu_custom_call" | custom-call | flops 4600000000 | tf_op jit(solution)/shard_map/pallas_call | solution.py:218
  13.6 0.0 collective-permute-done.1
  13.6 0.1 collective-permute-start.2
  13.7 1.8 %shard_map.57 = (f32[4,64,256]{2,1,0:T(8,128)S(1)}, f32[4,64,256]{2,1,0:T(8,128)S(1)}, f32[8,128]{1,0:T(8,128)S(1)}, f32[16,64,256]{2,1,0:T(8,128)S(1)}, f32[16,64,256]{2,1,0:T(8,128)S(1)}) custom-call(f32[16,64,256]{2,1,0:T(8,128)S(1)} %get-tuple-element.34.u.value, f32[3,16,64,256]{3,2,1,0:T(8,128)S(1)} %get-tuple-element.35.fp, ...), custom_call_target="tpu_custom_call" | custom-call | flops 3449999872 | tf_op jit(solution)/shard_map/pallas_call | solution.py:218
  15.5 0.0 collective-permute-done.2
  15.5 1.5 %collective-permute-start.3 = (f32[8,128]{1,0:T(8,128)S(1)}, f32[8,128]{1,0:T(8,128)S(1)}, u32[]{:S(2)}, u32[]{:S(2)}) collective-permute-start(f32[8,128]{1,0:T(8,128)S(1)} %maximum_maximum_fusion.1.dep), channel_id=1, source_target_pairs={{1,12},{5,14},{9,10},{13,6},{15,2},{11,0},{7,4},{3,8},{12,1},{14,5... | collective-permute-start | bytes 12296 | tf_op jit(solution)/shard_map/ppermute | solution.py:412
  17.0 0.0 collective-permute-done.4.near
  17.0 0.0 collective-permute-done.5.far
  17.0 2.1 %shard_map.58 = (f32[16,64,256]{2,1,0:T(8,128)S(1)}, f32[8,128]{1,0:T(8,128)S(1)}) custom-call(f32[16,64,256]{2,1,0:T(8,128)S(1)} %get-tuple-element.34.u.value, f32[3,64,256]{2,1,0:T(8,128)S(1)} %collective-permute-done.4.near, f32[3,64,256]{2,1,0:T(8,128)S(1)} %collective-permute-done.5.far, f32[3,16,64,256]{3,2,1,0:T(8,128)S(1)} %get-tuple-element.35.fp, ...), custom_call_target="tpu_custom_call" | custom-call | flops 2760000000 | tf_op jit(solution)/shard_map/pallas_call | solution.py:218
  19.1 1.4 %collective-permute-done.3 = f32[8,128]{1,0:T(8,128)S(1)} collective-permute-done((f32[8,128]{1,0:T(8,128)S(1)}, f32[8,128]{1,0:T(8,128)S(1)}, u32[]{:S(2)}, u32[]{:S(2)}) %collective-permute-start.3) | collective-permute-done | bytes 4128 | tf_op jit(solution)/shard_map/ppermute | solution.py:412
  20.4 0.5 %collective-permute-start.6 = (f32[8,128]{1,0:T(8,128)S(1)}, f32[8,128]{1,0:T(8,128)S(1)}, u32[]{:S(2)}, u32[]{:S(2)}) collective-permute-start(f32[8,128]{1,0:T(8,128)S(1)} %maximum_maximum_fusion.mine), channel_id=1, source_target_pairs={{0,1},{1,0},{2,3},{3,2},{4,5},{5,4},{6,7},{7,6},{8,9},{9,8},{10,11... | collective-permute-start | bytes 12296 | tf_op jit(solution)/shard_map/ppermute | solution.py:412
  20.9 0.8 %collective-permute-done.6.other = f32[8,128]{1,0:T(8,128)S(1)} collective-permute-done((f32[8,128]{1,0:T(8,128)S(1)}, f32[8,128]{1,0:T(8,128)S(1)}, u32[]{:S(2)}, u32[]{:S(2)}) %collective-permute-start.6) | collective-permute-done | bytes 4128 | tf_op jit(solution)/shard_map/ppermute | solution.py:412
  21.7 0.5 %shard_map.59 = (f32[16,64,256]{2,1,0:T(8,128)S(1)}, f32[8,128]{1,0:T(8,128)S(1)}, f32[3,64,256]{2,1,0:T(8,128)S(1)}, f32[3,64,256]{2,1,0:T(8,128)S(1)}) custom-call(f32[8,128]{1,0:T(8,128)S(1)} %maximum_maximum_fusion.mine, f32[8,128]{1,0:T(8,128)S(1)} %collective-permute-done.6.other, f32[16,64,256]{2,1,0:T(8,128)S(1)} %get-tuple-element.34.u.value, ...), custom_call_target="tpu_custom_call" | custom-call | flops 1150000000 | tf_op jit(solution)/shard_map/pallas_call | solution.py:218
  22.3 0.4 collective-permute-start.7
  22.7 2.1 %collective-permute-start.8 = (f32[3,64,256]{2,1,0:T(8,128)S(1)}, f32[3,64,256]{2,1,0:T(8,128)S(1)}, u32[]{:S(2)}, u32[]{:S(2)}) collective-permute-start(f32[3,64,256]{2,1,0:T(8,128)S(1)} %get-tuple-element.52), channel_id=1, source_target_pairs={{1,2},{3,4},{5,6},{7,8},{9,10},{11,12},{13,14},{15,0},{2,1},{4,3},... | collective-permute-start | bytes 589832 | tf_op jit(solution)/shard_map/ppermute | solution.py:412
  24.8 5.8 %shard_map.60 = (f32[16,64,256]{2,1,0:T(8,128)S(1)}, f32[16,64,256]{2,1,0:T(8,128)S(1)}, f32[8,128]{1,0:T(8,128)}) custom-call(f32[16,64,256]{2,1,0:T(8,128)S(1)} %get-tuple-element.50.u, f32[3,16,64,256]{3,2,1,0:T(8,128)S(1)} %get-tuple-element.35.fp, f32[3,16,64,256]{3,2,1,0:T(8,128)S(1)} %get-tuple-element.36.fm, ...), custom_call_target="tpu_custom_call" | custom-call | flops 6899999744 | tf_op jit(solution)/shard_map/pallas_call | solution.py:218
  30.6 0.0 collective-permute-done.7.near
  30.6 0.0 collective-permute-done.8.far
  30.6 2.4 %shard_map.61 = (f32[16,64,256]{2,1,0:T(8,128)S(1)}, f32[3,64,256]{2,1,0:T(8,128)S(1)}, f32[3,64,256]{2,1,0:T(8,128)S(1)}) custom-call(f32[16,64,256]{2,1,0:T(8,128)S(1)} %get-tuple-element.50.u, f32[3,64,256]{2,1,0:T(8,128)S(1)} %collective-permute-done.7.near, f32[3,64,256]{2,1,0:T(8,128)S(1)} %collective-permute-done.8.far, ...), custom_call_target="tpu_custom_call" | custom-call | flops 3449999872 | tf_op jit(solution)/shard_map/pallas_call | solution.py:218
  33.0 0.1 collective-permute-start.9
  33.1 2.4 %collective-permute-start.10 = (f32[3,64,256]{2,1,0:T(8,128)S(1)}, f32[3,64,256]{2,1,0:T(8,128)S(1)}, u32[]{:S(2)}, u32[]{:S(2)}) collective-permute-start(f32[3,64,256]{2,1,0:T(8,128)S(1)} %get-tuple-element.58), channel_id=1, source_target_pairs={{1,2},{3,4},{5,6},{7,8},{9,10},{11,12},{13,14},{15,0},{2,1},{4,3},... | collective-permute-start | bytes 589832 | tf_op jit(solution)/shard_map/ppermute | solution.py:412
  35.5 5.9 %shard_map.62 = (f32[16,64,256]{2,1,0:T(8,128)S(1)}, f32[16,64,256]{2,1,0:T(8,128)S(1)}, f32[8,128]{1,0:T(8,128)}) custom-call(f32[16,64,256]{2,1,0:T(8,128)S(1)} %get-tuple-element.56.u, f32[3,16,64,256]{3,2,1,0:T(8,128)S(1)} %get-tuple-element.35.fp, f32[3,16,64,256]{3,2,1,0:T(8,128)S(1)} %get-tuple-element.36.fm, ...), custom_call_target="tpu_custom_call" | custom-call | flops 6899999744 | tf_op jit(solution)/shard_map/pallas_call | solution.py:218
  41.3 0.0 collective-permute-done.9.near
  41.3 0.0 collective-permute-done.10.far
  41.4 3.1 %shard_map.63 = f32[16,64,256]{2,1,0:T(8,128)} custom-call(f32[16,64,256]{2,1,0:T(8,128)S(1)} %get-tuple-element.56.u, f32[3,64,256]{2,1,0:T(8,128)S(1)} %collective-permute-done.9.near, f32[3,64,256]{2,1,0:T(8,128)S(1)} %collective-permute-done.10.far, f32[8,128]{1,0:T(8,128)S(1)} %get-tuple-element.53.dep.kappa, ...), custom_call_target="tpu_custom_call" | custom-call | flops 3449999872 | tf_op jit(solution)/shard_map/pallas_call | solution.py:218
  (4 shorter events, 0.0 us)
Async XLA Ops:
  3.3 6.3 %collective-permute-start = (f32[8,128]{1,0:T(8,128)S(1)}, f32[8,128]{1,0:T(8,128)S(1)}, u32[]{:S(2)}, u32[]{:S(2)}) collective-permute-start(f32[8,128]{1,0:T(8,128)S(1)} %get-tuple-element.33), channel_id=1, source_target_pairs={{0,1},{1,0},{2,3},{3,2},{4,5},{5,4},{6,7},{7,6},{8,9},{9,8},{10,11... | collective-permute-start | bytes 12296 | tf_op jit(solution)/shard_map/ppermute | solution.py:412
  3.8 13.2 %collective-permute-start.4 = (f32[3,64,256]{2,1,0:T(8,128)S(1)}, f32[3,64,256]{2,1,0:T(8,128)S(1)}, u32[]{:S(2)}, u32[]{:S(2)}) collective-permute-start(f32[3,64,256]{2,1,0:T(8,128)S(1)} %get-tuple-element.40), channel_id=1, source_target_pairs={{0,1},{1,0},{2,3},{3,2},{4,5},{5,4},{6,7},{7,6},{8,9},{9,8},{10,11... | collective-permute-start | bytes 589832 | tf_op jit(solution)/shard_map/ppermute | solution.py:412
  3.9 13.1 %collective-permute-start.5 = (f32[3,64,256]{2,1,0:T(8,128)S(1)}, f32[3,64,256]{2,1,0:T(8,128)S(1)}, u32[]{:S(2)}, u32[]{:S(2)}) collective-permute-start(f32[3,64,256]{2,1,0:T(8,128)S(1)} %get-tuple-element.41), channel_id=1, source_target_pairs={{1,2},{3,4},{5,6},{7,8},{9,10},{11,12},{13,14},{15,0},{2,1},{4,3},... | collective-permute-start | bytes 589832 | tf_op jit(solution)/shard_map/ppermute | solution.py:412
  9.6 4.0 %collective-permute-start.1 = (f32[8,128]{1,0:T(8,128)S(1)}, f32[8,128]{1,0:T(8,128)S(1)}, u32[]{:S(2)}, u32[]{:S(2)}) collective-permute-start(f32[8,128]{1,0:T(8,128)S(1)} %max.21.dep), channel_id=1, source_target_pairs={{1,4},{5,8},{9,12},{13,14},{15,10},{11,6},{7,2},{3,0},{4,1},{8,5},... | collective-permute-start | bytes 12296 | tf_op jit(solution)/shard_map/ppermute | solution.py:412
  13.6 1.9 %collective-permute-start.2 = (f32[8,128]{1,0:T(8,128)S(1)}, f32[8,128]{1,0:T(8,128)S(1)}, u32[]{:S(2)}, u32[]{:S(2)}) collective-permute-start(f32[8,128]{1,0:T(8,128)S(1)} %maximum_maximum_fusion.2.dep), channel_id=1, source_target_pairs={{0,1},{1,0},{2,3},{3,2},{4,5},{5,4},{6,7},{7,6},{8,9},{9,8},{10,11... | collective-permute-start | bytes 12296 | tf_op jit(solution)/shard_map/ppermute | solution.py:412
  15.5 4.9 %collective-permute-start.3 = (f32[8,128]{1,0:T(8,128)S(1)}, f32[8,128]{1,0:T(8,128)S(1)}, u32[]{:S(2)}, u32[]{:S(2)}) collective-permute-start(f32[8,128]{1,0:T(8,128)S(1)} %maximum_maximum_fusion.1.dep), channel_id=1, source_target_pairs={{1,12},{5,14},{9,10},{13,6},{15,2},{11,0},{7,4},{3,8},{12,1},{14,5... | collective-permute-start | bytes 12296 | tf_op jit(solution)/shard_map/ppermute | solution.py:412
  20.4 1.3 %collective-permute-start.6 = (f32[8,128]{1,0:T(8,128)S(1)}, f32[8,128]{1,0:T(8,128)S(1)}, u32[]{:S(2)}, u32[]{:S(2)}) collective-permute-start(f32[8,128]{1,0:T(8,128)S(1)} %maximum_maximum_fusion.mine), channel_id=1, source_target_pairs={{0,1},{1,0},{2,3},{3,2},{4,5},{5,4},{6,7},{7,6},{8,9},{9,8},{10,11... | collective-permute-start | bytes 12296 | tf_op jit(solution)/shard_map/ppermute | solution.py:412
  22.3 8.3 %collective-permute-start.7 = (f32[3,64,256]{2,1,0:T(8,128)S(1)}, f32[3,64,256]{2,1,0:T(8,128)S(1)}, u32[]{:S(2)}, u32[]{:S(2)}) collective-permute-start(f32[3,64,256]{2,1,0:T(8,128)S(1)} %get-tuple-element.51), channel_id=1, source_target_pairs={{0,1},{1,0},{2,3},{3,2},{4,5},{5,4},{6,7},{7,6},{8,9},{9,8},{10,11... | collective-permute-start | bytes 589832 | tf_op jit(solution)/shard_map/ppermute | solution.py:412
  22.7 7.9 %collective-permute-start.8 = (f32[3,64,256]{2,1,0:T(8,128)S(1)}, f32[3,64,256]{2,1,0:T(8,128)S(1)}, u32[]{:S(2)}, u32[]{:S(2)}) collective-permute-start(f32[3,64,256]{2,1,0:T(8,128)S(1)} %get-tuple-element.52), channel_id=1, source_target_pairs={{1,2},{3,4},{5,6},{7,8},{9,10},{11,12},{13,14},{15,0},{2,1},{4,3},... | collective-permute-start | bytes 589832 | tf_op jit(solution)/shard_map/ppermute | solution.py:412
  33.0 8.4 %collective-permute-start.9 = (f32[3,64,256]{2,1,0:T(8,128)S(1)}, f32[3,64,256]{2,1,0:T(8,128)S(1)}, u32[]{:S(2)}, u32[]{:S(2)}) collective-permute-start(f32[3,64,256]{2,1,0:T(8,128)S(1)} %get-tuple-element.57), channel_id=1, source_target_pairs={{0,1},{1,0},{2,3},{3,2},{4,5},{5,4},{6,7},{7,6},{8,9},{9,8},{10,11... | collective-permute-start | bytes 589832 | tf_op jit(solution)/shard_map/ppermute | solution.py:412
  33.1 8.3 %collective-permute-start.10 = (f32[3,64,256]{2,1,0:T(8,128)S(1)}, f32[3,64,256]{2,1,0:T(8,128)S(1)}, u32[]{:S(2)}, u32[]{:S(2)}) collective-permute-start(f32[3,64,256]{2,1,0:T(8,128)S(1)} %get-tuple-element.58), channel_id=1, source_target_pairs={{1,2},{3,4},{5,6},{7,8},{9,10},{11,12},{13,14},{15,0},{2,1},{4,3},... | collective-permute-start | bytes 589832 | tf_op jit(solution)/shard_map/ppermute | solution.py:412

commit v4 on v3

--- a/solution.py
+++ b/solution.py
@@ -31,6 +31,14 @@
     m = base + g
     l = h + left
     r = h + right
+    return rcp(r * r), rcp(l * l), rcp(m * m * (1.0 / 6.0))
+
+
+def inverse_weights_direct(t, s0, s1):
+    base = t * t * (4.0 / 3.0) + 1e-6
+    m = base + s0 * s1
+    l = base + s0 * (s0 - t)
+    r = base + s1 * (s1 + t)
     return rcp(r * r), rcp(l * l), rcp(m * m * (1.0 / 6.0))
 
 
@@ -88,7 +96,7 @@
         s0, s1 = d1 - d0, d2 - d1
         t = s1 - s0
         wt[a:a + SUB] = t
-        r, l, m = inverse_weights(t, s0 * s1, twice_square(s0), twice_square(s1))
+        r, l, m = inverse_weights_direct(t, s0, s1)
         wr[a:a + SUB] = r
         wl[a:a + SUB] = l
         wm[a:a + SUB] = m
@@ -436,13 +444,13 @@
     mid = 2 * (3 * rows // 8)
     top = jnp.maximum(top, other)
     other = swap(top, ring(1))
-    ac0, bb0, done = rate_yz(vv, 0, mid, top, 4)
+    ac0, bb0, done, lo, hi = call(
+        functools.partial(yz_bounds_kernel, 0, mid), [VM] * 4 + [ANY, HBM, HBM],
+        [(VM, (mid, ny, nz))] * 2 + [(VM, tile)] + [(VM, flat)] * 2,
+        [pltpu.VMEM(flat, jnp.int32)] * 2 + [dma((2,))] + work, (vv,) + fields + (top, target, obstacle), 4)
     top = join(top, other, done)
     other = swap(top, pairs)
-    ac1, bb1, done, lo, hi = call(
-        functools.partial(yz_bounds_kernel, mid, rows), [VM] * 4 + [ANY, HBM, HBM],
-        [(VM, (rows - mid, ny, nz))] * 2 + [(VM, tile)] + [(VM, flat)] * 2,
-        [pltpu.VMEM(flat, jnp.int32)] * 2 + [dma((2,))] + work, (vv,) + fields + (top, target, obstacle), 3)
+    ac1, bb1, done = rate_yz(vv, mid, rows, top, 1.5)
     top = join(top, other, done)
     reach = 3
     other = swap(top, ring(reach))

time: 44.6 us -> 44.3 us (level)
  no operation moved by 1% of the time
where the time goes in v4:
time: 44.3 us; the launch traced here: 44.1 us
  Pallas kernels  28.5 us (64%)
  starting transfers between devices  13.3 us (30%)
  waiting for transfers between devices  2.2 us (5%)
    pallas_call x9, Pallas kernels, call(): pl.pallas_call(kernel, in_specs=ins, out_specs=[s for s, _ in outs], out_...  28.5 us
    ppermute x11, starting transfers between devices, swap(): return lax.ppermute(x, 'gx', perm)  13.3 us
    ppermute x11, waiting for transfers between devices, swap(): return lax.ppermute(x, 'gx', perm)  2.2 us
  transfers between devices with their start and end apart: 11, of which 2 were waited for; matrix products, arithmetic and copies ran while one was open for 0% of the time, Pallas kernels for 44%

profile of v4, /device:TPU:0, one launch (start us, length us, event | category | flops | bytes accessed | tf_op | source)
XLA Modules:
  0.0 44.1 jit_solution(167582350068993469)
XLA Ops:
  0.0 3.3 %shard_map.55 = (f32[3,16,64,256]{3,2,1,0:T(8,128)S(1)}, f32[3,16,64,256]{3,2,1,0:T(8,128)S(1)}, f32[3,16,64,256]{3,2,1,0:T(8,128)S(1)}, f32[16,64,256]{2,1,0:T(...) custom-call(f32[16,64,256]{2,1,0:T(8,128)} %value.1, ...), custom_call_target="tpu_custom_call" | custom-call | flops 3449999872 | tf_op jit(solution)/shard_map/pallas_call | solution.py:226
  3.3 0.5 %collective-permute-start = (f32[8,128]{1,0:T(8,128)S(1)}, f32[8,128]{1,0:T(8,128)S(1)}, u32[]{:S(2)}, u32[]{:S(2)}) collective-permute-start(f32[8,128]{1,0:T(8,128)S(1)} %get-tuple-element.33), channel_id=1, source_target_pairs={{0,1},{1,0},{2,3},{3,2},{4,5},{5,4},{6,7},{7,6},{8,9},{9,8},{10,11... | collective-permute-start | bytes 12296 | tf_op jit(solution)/shard_map/ppermute | solution.py:420
  3.8 0.1 collective-permute-start.4
  3.9 5.7 %collective-permute-start.5 = (f32[3,64,256]{2,1,0:T(8,128)S(1)}, f32[3,64,256]{2,1,0:T(8,128)S(1)}, u32[]{:S(2)}, u32[]{:S(2)}) collective-permute-start(f32[3,64,256]{2,1,0:T(8,128)S(1)} %get-tuple-element.41), channel_id=1, source_target_pairs={{1,2},{3,4},{5,6},{7,8},{9,10},{11,12},{13,14},{15,0},{2,1},{4,3},... | collective-permute-start | bytes 589832 | tf_op jit(solution)/shard_map/ppermute | solution.py:420
  9.6 0.0 collective-permute-done
  9.6 0.0 collective-permute-start.1
  9.6 4.2 %shard_map.56 = (f32[12,64,256]{2,1,0:T(8,128)S(1)}, f32[12,64,256]{2,1,0:T(8,128)S(1)}, f32[8,128]{1,0:T(8,128)S(1)}, f32[16,64,256]{2,1,0:T(8,128)S(1)}, f32[16,64,256]{2,1,0:T(8,128)S(1)}) custom-call(f32[16,64,256]{2,1,0:T(8,128)S(1)} %get-tuple-element.34.u.value, f32[3,16,64,256]{3,2,1,0:T(8,128)S(1)} %get-tuple-element.35.fp, ...), custom_call_target="tpu_custom_call" | custom-call | flops 4600000000 | tf_op jit(solution)/shard_map/pallas_call | solution.py:226
  13.8 0.0 collective-permute-done.1
  13.8 0.1 collective-permute-start.2
  13.9 1.3 %shard_map.57 = (f32[4,64,256]{2,1,0:T(8,128)S(1)}, f32[4,64,256]{2,1,0:T(8,128)S(1)}, f32[8,128]{1,0:T(8,128)S(1)}) custom-call(f32[16,64,256]{2,1,0:T(8,128)S(1)} %get-tuple-element.34.u.value, f32[3,16,64,256]{3,2,1,0:T(8,128)S(1)} %get-tuple-element.35.fp, f32[3,16,64,256]{3,2,1,0:T(8,128)S(1)} %get-tuple-element.36.fm, ...), custom_call_target="tpu_custom_call" | custom-call | flops 1724999936 | tf_op jit(solution)/shard_map/pallas_call | solution.py:226
  15.3 0.0 collective-permute-done.2
  15.3 1.5 %collective-permute-start.3 = (f32[8,128]{1,0:T(8,128)S(1)}, f32[8,128]{1,0:T(8,128)S(1)}, u32[]{:S(2)}, u32[]{:S(2)}) collective-permute-start(f32[8,128]{1,0:T(8,128)S(1)} %maximum_maximum_fusion.1.dep), channel_id=1, source_target_pairs={{1,12},{5,14},{9,10},{13,6},{15,2},{11,0},{7,4},{3,8},{12,1},{14,5... | collective-permute-start | bytes 12296 | tf_op jit(solution)/shard_map/ppermute | solution.py:420
  16.7 0.0 collective-permute-done.4.near
  16.7 0.0 collective-permute-done.5.far
  16.7 2.1 %shard_map.58 = (f32[16,64,256]{2,1,0:T(8,128)S(1)}, f32[8,128]{1,0:T(8,128)S(1)}) custom-call(f32[16,64,256]{2,1,0:T(8,128)S(1)} %get-tuple-element.34.u.value, f32[3,64,256]{2,1,0:T(8,128)S(1)} %collective-permute-done.4.near, f32[3,64,256]{2,1,0:T(8,128)S(1)} %collective-permute-done.5.far, f32[3,16,64,256]{3,2,1,0:T(8,128)S(1)} %get-tuple-element.35.fp, ...), custom_call_target="tpu_custom_call" | custom-call | flops 2760000000 | tf_op jit(solution)/shard_map/pallas_call | solution.py:226
  18.8 1.4 %collective-permute-done.3 = f32[8,128]{1,0:T(8,128)S(1)} collective-permute-done((f32[8,128]{1,0:T(8,128)S(1)}, f32[8,128]{1,0:T(8,128)S(1)}, u32[]{:S(2)}, u32[]{:S(2)}) %collective-permute-start.3) | collective-permute-done | bytes 4128 | tf_op jit(solution)/shard_map/ppermute | solution.py:420
  20.2 0.5 %collective-permute-start.6 = (f32[8,128]{1,0:T(8,128)S(1)}, f32[8,128]{1,0:T(8,128)S(1)}, u32[]{:S(2)}, u32[]{:S(2)}) collective-permute-start(f32[8,128]{1,0:T(8,128)S(1)} %maximum_maximum_fusion.mine), channel_id=1, source_target_pairs={{0,1},{1,0},{2,3},{3,2},{4,5},{5,4},{6,7},{7,6},{8,9},{9,8},{10,11... | collective-permute-start | bytes 12296 | tf_op jit(solution)/shard_map/ppermute | solution.py:420
  20.7 0.8 %collective-permute-done.6.other = f32[8,128]{1,0:T(8,128)S(1)} collective-permute-done((f32[8,128]{1,0:T(8,128)S(1)}, f32[8,128]{1,0:T(8,128)S(1)}, u32[]{:S(2)}, u32[]{:S(2)}) %collective-permute-start.6) | collective-permute-done | bytes 4128 | tf_op jit(solution)/shard_map/ppermute | solution.py:420
  21.5 0.5 %shard_map.59 = (f32[16,64,256]{2,1,0:T(8,128)S(1)}, f32[8,128]{1,0:T(8,128)S(1)}, f32[3,64,256]{2,1,0:T(8,128)S(1)}, f32[3,64,256]{2,1,0:T(8,128)S(1)}) custom-call(f32[8,128]{1,0:T(8,128)S(1)} %maximum_maximum_fusion.mine, f32[8,128]{1,0:T(8,128)S(1)} %collective-permute-done.6.other, f32[16,64,256]{2,1,0:T(8,128)S(1)} %get-tuple-element.34.u.value, ...), custom_call_target="tpu_custom_call" | custom-call | flops 1150000000 | tf_op jit(solution)/shard_map/pallas_call | solution.py:226
  22.0 0.4 collective-permute-start.7
  22.4 2.1 %collective-permute-start.8 = (f32[3,64,256]{2,1,0:T(8,128)S(1)}, f32[3,64,256]{2,1,0:T(8,128)S(1)}, u32[]{:S(2)}, u32[]{:S(2)}) collective-permute-start(f32[3,64,256]{2,1,0:T(8,128)S(1)} %get-tuple-element.52), channel_id=1, source_target_pairs={{1,2},{3,4},{5,6},{7,8},{9,10},{11,12},{13,14},{15,0},{2,1},{4,3},... | collective-permute-start | bytes 589832 | tf_op jit(solution)/shard_map/ppermute | solution.py:420
  24.5 5.8 %shard_map.60 = (f32[16,64,256]{2,1,0:T(8,128)S(1)}, f32[16,64,256]{2,1,0:T(8,128)S(1)}, f32[8,128]{1,0:T(8,128)}) custom-call(f32[16,64,256]{2,1,0:T(8,128)S(1)} %get-tuple-element.50.u, f32[3,16,64,256]{3,2,1,0:T(8,128)S(1)} %get-tuple-element.35.fp, f32[3,16,64,256]{3,2,1,0:T(8,128)S(1)} %get-tuple-element.36.fm, ...), custom_call_target="tpu_custom_call" | custom-call | flops 6899999744 | tf_op jit(solution)/shard_map/pallas_call | solution.py:226
  30.3 0.0 collective-permute-done.7.near
  30.3 0.0 collective-permute-done.8.far
  30.3 2.4 %shard_map.61 = (f32[16,64,256]{2,1,0:T(8,128)S(1)}, f32[3,64,256]{2,1,0:T(8,128)S(1)}, f32[3,64,256]{2,1,0:T(8,128)S(1)}) custom-call(f32[16,64,256]{2,1,0:T(8,128)S(1)} %get-tuple-element.50.u, f32[3,64,256]{2,1,0:T(8,128)S(1)} %collective-permute-done.7.near, f32[3,64,256]{2,1,0:T(8,128)S(1)} %collective-permute-done.8.far, ...), custom_call_target="tpu_custom_call" | custom-call | flops 3449999872 | tf_op jit(solution)/shard_map/pallas_call | solution.py:226
  32.7 0.1 collective-permute-start.9
  32.8 2.4 %collective-permute-start.10 = (f32[3,64,256]{2,1,0:T(8,128)S(1)}, f32[3,64,256]{2,1,0:T(8,128)S(1)}, u32[]{:S(2)}, u32[]{:S(2)}) collective-permute-start(f32[3,64,256]{2,1,0:T(8,128)S(1)} %get-tuple-element.58), channel_id=1, source_target_pairs={{1,2},{3,4},{5,6},{7,8},{9,10},{11,12},{13,14},{15,0},{2,1},{4,3},... | collective-permute-start | bytes 589832 | tf_op jit(solution)/shard_map/ppermute | solution.py:420
  35.2 5.8 %shard_map.62 = (f32[16,64,256]{2,1,0:T(8,128)S(1)}, f32[16,64,256]{2,1,0:T(8,128)S(1)}, f32[8,128]{1,0:T(8,128)}) custom-call(f32[16,64,256]{2,1,0:T(8,128)S(1)} %get-tuple-element.56.u, f32[3,16,64,256]{3,2,1,0:T(8,128)S(1)} %get-tuple-element.35.fp, f32[3,16,64,256]{3,2,1,0:T(8,128)S(1)} %get-tuple-element.36.fm, ...), custom_call_target="tpu_custom_call" | custom-call | flops 6899999744 | tf_op jit(solution)/shard_map/pallas_call | solution.py:226
  41.1 0.0 collective-permute-done.9.near
  41.1 0.0 collective-permute-done.10.far
  41.1 3.1 %shard_map.63 = f32[16,64,256]{2,1,0:T(8,128)} custom-call(f32[16,64,256]{2,1,0:T(8,128)S(1)} %get-tuple-element.56.u, f32[3,64,256]{2,1,0:T(8,128)S(1)} %collective-permute-done.9.near, f32[3,64,256]{2,1,0:T(8,128)S(1)} %collective-permute-done.10.far, f32[8,128]{1,0:T(8,128)S(1)} %get-tuple-element.53.dep.kappa, ...), custom_call_target="tpu_custom_call" | custom-call | flops 3449999872 | tf_op jit(solution)/shard_map/pallas_call | solution.py:226
  (4 shorter events, 0.0 us)
Async XLA Ops:
  3.3 6.3 %collective-permute-start = (f32[8,128]{1,0:T(8,128)S(1)}, f32[8,128]{1,0:T(8,128)S(1)}, u32[]{:S(2)}, u32[]{:S(2)}) collective-permute-start(f32[8,128]{1,0:T(8,128)S(1)} %get-tuple-element.33), channel_id=1, source_target_pairs={{0,1},{1,0},{2,3},{3,2},{4,5},{5,4},{6,7},{7,6},{8,9},{9,8},{10,11... | collective-permute-start | bytes 12296 | tf_op jit(solution)/shard_map/ppermute | solution.py:420
  3.8 12.9 %collective-permute-start.4 = (f32[3,64,256]{2,1,0:T(8,128)S(1)}, f32[3,64,256]{2,1,0:T(8,128)S(1)}, u32[]{:S(2)}, u32[]{:S(2)}) collective-permute-start(f32[3,64,256]{2,1,0:T(8,128)S(1)} %get-tuple-element.40), channel_id=1, source_target_pairs={{0,1},{1,0},{2,3},{3,2},{4,5},{5,4},{6,7},{7,6},{8,9},{9,8},{10,11... | collective-permute-start | bytes 589832 | tf_op jit(solution)/shard_map/ppermute | solution.py:420
  3.9 12.8 %collective-permute-start.5 = (f32[3,64,256]{2,1,0:T(8,128)S(1)}, f32[3,64,256]{2,1,0:T(8,128)S(1)}, u32[]{:S(2)}, u32[]{:S(2)}) collective-permute-start(f32[3,64,256]{2,1,0:T(8,128)S(1)} %get-tuple-element.41), channel_id=1, source_target_pairs={{1,2},{3,4},{5,6},{7,8},{9,10},{11,12},{13,14},{15,0},{2,1},{4,3},... | collective-permute-start | bytes 589832 | tf_op jit(solution)/shard_map/ppermute | solution.py:420
  9.6 4.3 %collective-permute-start.1 = (f32[8,128]{1,0:T(8,128)S(1)}, f32[8,128]{1,0:T(8,128)S(1)}, u32[]{:S(2)}, u32[]{:S(2)}) collective-permute-start(f32[8,128]{1,0:T(8,128)S(1)} %max.21.dep), channel_id=1, source_target_pairs={{1,4},{5,8},{9,12},{13,14},{15,10},{11,6},{7,2},{3,0},{4,1},{8,5},... | collective-permute-start | bytes 12296 | tf_op jit(solution)/shard_map/ppermute | solution.py:420
  13.8 1.4 %collective-permute-start.2 = (f32[8,128]{1,0:T(8,128)S(1)}, f32[8,128]{1,0:T(8,128)S(1)}, u32[]{:S(2)}, u32[]{:S(2)}) collective-permute-start(f32[8,128]{1,0:T(8,128)S(1)} %maximum_maximum_fusion.2.dep), channel_id=1, source_target_pairs={{0,1},{1,0},{2,3},{3,2},{4,5},{5,4},{6,7},{7,6},{8,9},{9,8},{10,11... | collective-permute-start | bytes 12296 | tf_op jit(solution)/shard_map/ppermute | solution.py:420
  15.3 4.9 %collective-permute-start.3 = (f32[8,128]{1,0:T(8,128)S(1)}, f32[8,128]{1,0:T(8,128)S(1)}, u32[]{:S(2)}, u32[]{:S(2)}) collective-permute-start(f32[8,128]{1,0:T(8,128)S(1)} %maximum_maximum_fusion.1.dep), channel_id=1, source_target_pairs={{1,12},{5,14},{9,10},{13,6},{15,2},{11,0},{7,4},{3,8},{12,1},{14,5... | collective-permute-start | bytes 12296 | tf_op jit(solution)/shard_map/ppermute | solution.py:420
  20.2 1.3 %collective-permute-start.6 = (f32[8,128]{1,0:T(8,128)S(1)}, f32[8,128]{1,0:T(8,128)S(1)}, u32[]{:S(2)}, u32[]{:S(2)}) collective-permute-start(f32[8,128]{1,0:T(8,128)S(1)} %maximum_maximum_fusion.mine), channel_id=1, source_target_pairs={{0,1},{1,0},{2,3},{3,2},{4,5},{5,4},{6,7},{7,6},{8,9},{9,8},{10,11... | collective-permute-start | bytes 12296 | tf_op jit(solution)/shard_map/ppermute | solution.py:420
  22.0 8.3 %collective-permute-start.7 = (f32[3,64,256]{2,1,0:T(8,128)S(1)}, f32[3,64,256]{2,1,0:T(8,128)S(1)}, u32[]{:S(2)}, u32[]{:S(2)}) collective-permute-start(f32[3,64,256]{2,1,0:T(8,128)S(1)} %get-tuple-element.51), channel_id=1, source_target_pairs={{0,1},{1,0},{2,3},{3,2},{4,5},{5,4},{6,7},{7,6},{8,9},{9,8},{10,11... | collective-permute-start | bytes 589832 | tf_op jit(solution)/shard_map/ppermute | solution.py:420
  22.4 7.9 %collective-permute-start.8 = (f32[3,64,256]{2,1,0:T(8,128)S(1)}, f32[3,64,256]{2,1,0:T(8,128)S(1)}, u32[]{:S(2)}, u32[]{:S(2)}) collective-permute-start(f32[3,64,256]{2,1,0:T(8,128)S(1)} %get-tuple-element.52), channel_id=1, source_target_pairs={{1,2},{3,4},{5,6},{7,8},{9,10},{11,12},{13,14},{15,0},{2,1},{4,3},... | collective-permute-start | bytes 589832 | tf_op jit(solution)/shard_map/ppermute | solution.py:420
  32.7 8.3 %collective-permute-start.9 = (f32[3,64,256]{2,1,0:T(8,128)S(1)}, f32[3,64,256]{2,1,0:T(8,128)S(1)}, u32[]{:S(2)}, u32[]{:S(2)}) collective-permute-start(f32[3,64,256]{2,1,0:T(8,128)S(1)} %get-tuple-element.57), channel_id=1, source_target_pairs={{0,1},{1,0},{2,3},{3,2},{4,5},{5,4},{6,7},{7,6},{8,9},{9,8},{10,11... | collective-permute-start | bytes 589832 | tf_op jit(solution)/shard_map/ppermute | solution.py:420
  32.8 8.2 %collective-permute-start.10 = (f32[3,64,256]{2,1,0:T(8,128)S(1)}, f32[3,64,256]{2,1,0:T(8,128)S(1)}, u32[]{:S(2)}, u32[]{:S(2)}) collective-permute-start(f32[3,64,256]{2,1,0:T(8,128)S(1)} %get-tuple-element.58), channel_id=1, source_target_pairs={{1,2},{3,4},{5,6},{7,8},{9,10},{11,12},{13,14},{15,0},{2,1},{4,3},... | collective-permute-start | bytes 589832 | tf_op jit(solution)/shard_map/ppermute | solution.py:420

commit v5 on v4

--- a/solution.py
+++ b/solution.py
@@ -238,14 +238,16 @@
     last = u.shape[0] - 3
 
     def body(r, _):
-        near[r] = u[(1 - odd) * last + r]
-        far[r] = u[odd * last + r]
+        if near is not None:
+            near[r] = u[(1 - odd) * last + r]
+        if far is not None:
+            far[r] = u[odd * last + r]
         return 0
 
     lax.fori_loop(0, 3, body, 0)
 
 
-def prep_kernel(chunk, value, drift, gain, fp, fm, gv, vv, near, far, top, dv, sems, gsems, vsem):
+def prep_kernel(chunk, value, drift, gain, fp, fm, gv, vv, far, top, dv, sems, gsems, vsem):
     rows, ny, nz = value.shape
     n = rows // chunk
     moves = []
@@ -281,7 +283,7 @@
         best = lax.fori_loop(0, chunk * (ny // SUB), body, best, unroll=4)
     top[...] = best
     keep.wait()
-    send_rows(vv, parity(), near, far)
+    send_rows(vv, parity(), None, far)
 
 
 def yz_bounds_kernel(first, last, u, fp, fm, gain, dep, target, obstacle, ac, bb, done, lo, hi, tv, ov, sems, *scratch):
@@ -300,6 +302,12 @@
         return 0
 
     lax.fori_loop(0, u.shape[0], body, 0)
+
+
+def yz_send_kernel(first, last, u, fp, fm, gain, dep, ac, bb, done, near, *scratch):
+    send_rows(u, parity(), near, None)
+    yz_pass(u, (fp, fm, gain), ac, bb, scratch, first, last)
+    done[...] = jnp.zeros_like(done)
 
 
 def yz_kernel(first, last, u, fp, fm, gain, dep, ac, bb, done, *scratch):
@@ -421,17 +429,16 @@
 
     chunk = 2
     dma = pltpu.SemaphoreType.DMA
-    fp, fm, gv, vv, near, far, top = call(
+    fp, fm, gv, vv, far, top = call(
         functools.partial(prep_kernel, chunk),
         [HBM, HBM, HBM],
-        [(VM, deep)] * 3 + [(VM, flat), (VM, ends), (VM, ends), (VM, tile)],
+        [(VM, deep)] * 3 + [(VM, flat), (VM, ends), (VM, tile)],
         [pltpu.VMEM(deep, F32)] + [dma((rows // chunk,))] * 2 + [dma((1,))],
         (value, drift, gain), 3)
     fields = (fp, fm, gv)
     work = yz_scratch(ny, nz)
     other = swap(top, pairs)
     far = swap(far, links)
-    near = swap(near, pairs)
 
     def join(top, other, done):
         return jnp.maximum(jnp.maximum(top, other), done)
@@ -450,7 +457,10 @@
         [pltpu.VMEM(flat, jnp.int32)] * 2 + [dma((2,))] + work, (vv,) + fields + (top, target, obstacle), 4)
     top = join(top, other, done)
     other = swap(top, pairs)
-    ac1, bb1, done = rate_yz(vv, mid, rows, top, 1.5)
+    ac1, bb1, done, near = call(
+        functools.partial(yz_send_kernel, mid, rows), [VM] * 4 + [ANY],
+        [(VM, (rows - mid, ny, nz))] * 2 + [(VM, tile), (VM, ends)], work, (vv,) + fields + (top,), 1.5)
+    near = swap(near, pairs)
     top = join(top, other, done)
     reach = 3
     other = swap(top, ring(reach))

time: 44.3 us -> 44.3 us (level)
  waiting for transfers between devices: 2.2 us -> 2.75 us
  starting transfers between devices: 13.3 us -> 12.8 us
    ppermute x11, waiting for transfers between devices: 2.2 us -> 2.75 us  [swap(): return lax.ppermute(x, 'gx', perm)]
    ppermute x11, starting transfers between devices: 13.3 us -> 12.8 us  [swap(): return lax.ppermute(x, 'gx', perm)]
where the time goes in v5:
time: 44.3 us; the launch traced here: 44.2 us
  Pallas kernels  28.5 us (64%)
  starting transfers between devices  12.8 us (29%)
  waiting for transfers between devices  2.75 us (6%)
    pallas_call x9, Pallas kernels, call(): pl.pallas_call(kernel, in_specs=ins, out_specs=[s for s, _ in outs], out_...  28.5 us
    ppermute x11, starting transfers between devices, swap(): return lax.ppermute(x, 'gx', perm)  12.8 us
    ppermute x11, waiting for transfers between devices, swap(): return lax.ppermute(x, 'gx', perm)  2.75 us
  transfers between devices with their start and end apart: 11, of which 2 were waited for; matrix products, arithmetic and copies ran while one was open for 0% of the time, Pallas kernels for 44%

profile of v5, /device:TPU:0, one launch (start us, length us, event | category | flops | bytes accessed | tf_op | source)
XLA Modules:
  0.0 44.2 jit_solution(13894383635428647227)
XLA Ops:
  0.0 3.3 %shard_map.55 = (f32[3,16,64,256]{3,2,1,0:T(8,128)S(1)}, f32[3,16,64,256]{3,2,1,0:T(8,128)S(1)}, f32[3,16,64,256]{3,2,1,0:T(8,128)S(1)}, f32[16,64,256]{2,1,0:T(...) custom-call(f32[16,64,256]{2,1,0:T(8,128)} %value.1, f32[3,16,64,256]{3,2,1,0:T(8,128)} %drift.1, ...), custom_call_target="tpu_custom_call" | custom-call | flops 3449999872 | tf_op jit(solution)/shard_map/pallas_call | solution.py:226
  3.3 0.5 %collective-permute-start = (f32[8,128]{1,0:T(8,128)S(1)}, f32[8,128]{1,0:T(8,128)S(1)}, u32[]{:S(2)}, u32[]{:S(2)}) collective-permute-start(f32[8,128]{1,0:T(8,128)S(1)} %get-tuple-element.33), channel_id=1, source_target_pairs={{0,1},{1,0},{2,3},{3,2},{4,5},{5,4},{6,7},{7,6},{8,9},{9,8},{10,11... | collective-permute-start | bytes 12296 | tf_op jit(solution)/shard_map/ppermute | solution.py:428
  3.8 5.7 %collective-permute-start.5 = (f32[3,64,256]{2,1,0:T(8,128)S(1)}, f32[3,64,256]{2,1,0:T(8,128)S(1)}, u32[]{:S(2)}, u32[]{:S(2)}) collective-permute-start(f32[3,64,256]{2,1,0:T(8,128)S(1)} %get-tuple-element.41), channel_id=1, source_target_pairs={{1,2},{3,4},{5,6},{7,8},{9,10},{11,12},{13,14},{15,0},{2,1},{4,3},... | collective-permute-start | bytes 589832 | tf_op jit(solution)/shard_map/ppermute | solution.py:428
  9.5 0.0 collective-permute-done
  9.5 0.0 collective-permute-start.1
  9.5 4.2 %shard_map.56 = (f32[12,64,256]{2,1,0:T(8,128)S(1)}, f32[12,64,256]{2,1,0:T(8,128)S(1)}, f32[8,128]{1,0:T(8,128)S(1)}, f32[16,64,256]{2,1,0:T(8,128)S(1)}, f32[16,64,256]{2,1,0:T(8,128)S(1)}) custom-call(f32[16,64,256]{2,1,0:T(8,128)S(1)} %get-tuple-element.34.u.value, f32[3,16,64,256]{3,2,1,0:T(8,128)S(1)} %get-tuple-element.35.fp, ...), custom_call_target="tpu_custom_call" | custom-call | flops 4600000000 | tf_op jit(solution)/shard_map/pallas_call | solution.py:226
  13.7 0.0 collective-permute-done.1
  13.8 0.1 collective-permute-start.2
  13.8 1.4 %shard_map.57 = (f32[4,64,256]{2,1,0:T(8,128)S(1)}, f32[4,64,256]{2,1,0:T(8,128)S(1)}, f32[8,128]{1,0:T(8,128)S(1)}, f32[3,64,256]{2,1,0:T(8,128)S(1)}) custom-call(f32[16,64,256]{2,1,0:T(8,128)S(1)} %get-tuple-element.34.u.value, f32[3,16,64,256]{3,2,1,0:T(8,128)S(1)} %get-tuple-element.35.fp, f32[3,16,64,256]{3,2,1,0:T(8,128)S(1)} %get-tuple-element.36.fm, ...), custom_call_target="tpu_custom_call" | custom-call | flops 1724999936 | tf_op jit(solution)/shard_map/pallas_call | solution.py:226
  15.2 0.5 %collective-permute-start.4 = (f32[3,64,256]{2,1,0:T(8,128)S(1)}, f32[3,64,256]{2,1,0:T(8,128)S(1)}, u32[]{:S(2)}, u32[]{:S(2)}) collective-permute-start(f32[3,64,256]{2,1,0:T(8,128)S(1)} %get-tuple-element.40), channel_id=1, source_target_pairs={{0,1},{1,0},{2,3},{3,2},{4,5},{5,4},{6,7},{7,6},{8,9},{9,8},{10,11... | collective-permute-start | bytes 589832 | tf_op jit(solution)/shard_map/ppermute | solution.py:428
  15.7 0.0 collective-permute-done.2
  15.7 1.1 %collective-permute-start.3 = (f32[8,128]{1,0:T(8,128)S(1)}, f32[8,128]{1,0:T(8,128)S(1)}, u32[]{:S(2)}, u32[]{:S(2)}) collective-permute-start(f32[8,128]{1,0:T(8,128)S(1)} %maximum_maximum_fusion.1.dep), channel_id=1, source_target_pairs={{1,12},{5,14},{9,10},{13,6},{15,2},{11,0},{7,4},{3,8},{12,1},{14,5... | collective-permute-start | bytes 12296 | tf_op jit(solution)/shard_map/ppermute | solution.py:428
  16.8 0.0 collective-permute-done.5.far
  16.8 0.0 collective-permute-done.4.near
  16.8 2.1 %shard_map.58 = (f32[16,64,256]{2,1,0:T(8,128)S(1)}, f32[8,128]{1,0:T(8,128)S(1)}) custom-call(f32[16,64,256]{2,1,0:T(8,128)S(1)} %get-tuple-element.34.u.value, f32[3,64,256]{2,1,0:T(8,128)S(1)} %collective-permute-done.4.near, f32[3,64,256]{2,1,0:T(8,128)S(1)} %collective-permute-done.5.far, f32[3,16,64,256]{3,2,1,0:T(8,128)S(1)} %get-tuple-element.35.fp, ...), custom_call_target="tpu_custom_call" | custom-call | flops 2760000000 | tf_op jit(solution)/shard_map/pallas_call | solution.py:226
  18.9 1.7 %collective-permute-done.3 = f32[8,128]{1,0:T(8,128)S(1)} collective-permute-done((f32[8,128]{1,0:T(8,128)S(1)}, f32[8,128]{1,0:T(8,128)S(1)}, u32[]{:S(2)}, u32[]{:S(2)}) %collective-permute-start.3) | collective-permute-done | bytes 4128 | tf_op jit(solution)/shard_map/ppermute | solution.py:428
  20.6 0.1 collective-permute-start.6
  20.7 1.1 %collective-permute-done.6.other = f32[8,128]{1,0:T(8,128)S(1)} collective-permute-done((f32[8,128]{1,0:T(8,128)S(1)}, f32[8,128]{1,0:T(8,128)S(1)}, u32[]{:S(2)}, u32[]{:S(2)}) %collective-permute-start.6) | collective-permute-done | bytes 4128 | tf_op jit(solution)/shard_map/ppermute | solution.py:428
  21.8 0.5 %shard_map.59 = (f32[16,64,256]{2,1,0:T(8,128)S(1)}, f32[8,128]{1,0:T(8,128)S(1)}, f32[3,64,256]{2,1,0:T(8,128)S(1)}, f32[3,64,256]{2,1,0:T(8,128)S(1)}) custom-call(f32[8,128]{1,0:T(8,128)S(1)} %maximum_maximum_fusion.mine, f32[8,128]{1,0:T(8,128)S(1)} %collective-permute-done.6.other, f32[16,64,256]{2,1,0:T(8,128)S(1)} %get-tuple-element.34.u.value, ...), custom_call_target="tpu_custom_call" | custom-call | flops 1150000000 | tf_op jit(solution)/shard_map/pallas_call | solution.py:226
  22.2 0.2 collective-permute-start.7
  22.5 2.0 %collective-permute-start.8 = (f32[3,64,256]{2,1,0:T(8,128)S(1)}, f32[3,64,256]{2,1,0:T(8,128)S(1)}, u32[]{:S(2)}, u32[]{:S(2)}) collective-permute-start(f32[3,64,256]{2,1,0:T(8,128)S(1)} %get-tuple-element.52), channel_id=1, source_target_pairs={{1,2},{3,4},{5,6},{7,8},{9,10},{11,12},{13,14},{15,0},{2,1},{4,3},... | collective-permute-start | bytes 589832 | tf_op jit(solution)/shard_map/ppermute | solution.py:428
  24.5 5.8 %shard_map.60 = (f32[16,64,256]{2,1,0:T(8,128)S(1)}, f32[16,64,256]{2,1,0:T(8,128)S(1)}, f32[8,128]{1,0:T(8,128)}) custom-call(f32[16,64,256]{2,1,0:T(8,128)S(1)} %get-tuple-element.50.u, f32[3,16,64,256]{3,2,1,0:T(8,128)S(1)} %get-tuple-element.35.fp, f32[3,16,64,256]{3,2,1,0:T(8,128)S(1)} %get-tuple-element.36.fm, ...), custom_call_target="tpu_custom_call" | custom-call | flops 6899999744 | tf_op jit(solution)/shard_map/pallas_call | solution.py:226
  30.3 0.0 collective-permute-done.7.near
  30.3 0.0 collective-permute-done.8.far
  30.3 2.4 %shard_map.61 = (f32[16,64,256]{2,1,0:T(8,128)S(1)}, f32[3,64,256]{2,1,0:T(8,128)S(1)}, f32[3,64,256]{2,1,0:T(8,128)S(1)}) custom-call(f32[16,64,256]{2,1,0:T(8,128)S(1)} %get-tuple-element.50.u, f32[3,64,256]{2,1,0:T(8,128)S(1)} %collective-permute-done.7.near, f32[3,64,256]{2,1,0:T(8,128)S(1)} %collective-permute-done.8.far, ...), custom_call_target="tpu_custom_call" | custom-call | flops 3449999872 | tf_op jit(solution)/shard_map/pallas_call | solution.py:226
  32.7 0.1 collective-permute-start.9
  32.8 2.4 %collective-permute-start.10 = (f32[3,64,256]{2,1,0:T(8,128)S(1)}, f32[3,64,256]{2,1,0:T(8,128)S(1)}, u32[]{:S(2)}, u32[]{:S(2)}) collective-permute-start(f32[3,64,256]{2,1,0:T(8,128)S(1)} %get-tuple-element.58), channel_id=1, source_target_pairs={{1,2},{3,4},{5,6},{7,8},{9,10},{11,12},{13,14},{15,0},{2,1},{4,3},... | collective-permute-start | bytes 589832 | tf_op jit(solution)/shard_map/ppermute | solution.py:428
  35.2 5.8 %shard_map.62 = (f32[16,64,256]{2,1,0:T(8,128)S(1)}, f32[16,64,256]{2,1,0:T(8,128)S(1)}, f32[8,128]{1,0:T(8,128)}) custom-call(f32[16,64,256]{2,1,0:T(8,128)S(1)} %get-tuple-element.56.u, f32[3,16,64,256]{3,2,1,0:T(8,128)S(1)} %get-tuple-element.35.fp, f32[3,16,64,256]{3,2,1,0:T(8,128)S(1)} %get-tuple-element.36.fm, ...), custom_call_target="tpu_custom_call" | custom-call | flops 6899999744 | tf_op jit(solution)/shard_map/pallas_call | solution.py:226
  41.1 0.0 collective-permute-done.9.near
  41.1 0.0 collective-permute-done.10.far
  41.1 3.1 %shard_map.63 = f32[16,64,256]{2,1,0:T(8,128)} custom-call(f32[16,64,256]{2,1,0:T(8,128)S(1)} %get-tuple-element.56.u, f32[3,64,256]{2,1,0:T(8,128)S(1)} %collective-permute-done.9.near, f32[3,64,256]{2,1,0:T(8,128)S(1)} %collective-permute-done.10.far, f32[8,128]{1,0:T(8,128)S(1)} %get-tuple-element.53.dep.kappa, ...), custom_call_target="tpu_custom_call" | custom-call | flops 3449999872 | tf_op jit(solution)/shard_map/pallas_call | solution.py:226
  (4 shorter events, 0.0 us)
Async XLA Ops:
  3.3 6.2 %collective-permute-start = (f32[8,128]{1,0:T(8,128)S(1)}, f32[8,128]{1,0:T(8,128)S(1)}, u32[]{:S(2)}, u32[]{:S(2)}) collective-permute-start(f32[8,128]{1,0:T(8,128)S(1)} %get-tuple-element.33), channel_id=1, source_target_pairs={{0,1},{1,0},{2,3},{3,2},{4,5},{5,4},{6,7},{7,6},{8,9},{9,8},{10,11... | collective-permute-start | bytes 12296 | tf_op jit(solution)/shard_map/ppermute | solution.py:428
  3.8 13.0 %collective-permute-start.5 = (f32[3,64,256]{2,1,0:T(8,128)S(1)}, f32[3,64,256]{2,1,0:T(8,128)S(1)}, u32[]{:S(2)}, u32[]{:S(2)}) collective-permute-start(f32[3,64,256]{2,1,0:T(8,128)S(1)} %get-tuple-element.41), channel_id=1, source_target_pairs={{1,2},{3,4},{5,6},{7,8},{9,10},{11,12},{13,14},{15,0},{2,1},{4,3},... | collective-permute-start | bytes 589832 | tf_op jit(solution)/shard_map/ppermute | solution.py:428
  9.5 4.3 %collective-permute-start.1 = (f32[8,128]{1,0:T(8,128)S(1)}, f32[8,128]{1,0:T(8,128)S(1)}, u32[]{:S(2)}, u32[]{:S(2)}) collective-permute-start(f32[8,128]{1,0:T(8,128)S(1)} %max.21.dep), channel_id=1, source_target_pairs={{1,4},{5,8},{9,12},{13,14},{15,10},{11,6},{7,2},{3,0},{4,1},{8,5},... | collective-permute-start | bytes 12296 | tf_op jit(solution)/shard_map/ppermute | solution.py:428
  13.8 2.0 %collective-permute-start.2 = (f32[8,128]{1,0:T(8,128)S(1)}, f32[8,128]{1,0:T(8,128)S(1)}, u32[]{:S(2)}, u32[]{:S(2)}) collective-permute-start(f32[8,128]{1,0:T(8,128)S(1)} %maximum_maximum_fusion.2.dep), channel_id=1, source_target_pairs={{0,1},{1,0},{2,3},{3,2},{4,5},{5,4},{6,7},{7,6},{8,9},{9,8},{10,11... | collective-permute-start | bytes 12296 | tf_op jit(solution)/shard_map/ppermute | solution.py:428
  15.2 1.6 %collective-permute-start.4 = (f32[3,64,256]{2,1,0:T(8,128)S(1)}, f32[3,64,256]{2,1,0:T(8,128)S(1)}, u32[]{:S(2)}, u32[]{:S(2)}) collective-permute-start(f32[3,64,256]{2,1,0:T(8,128)S(1)} %get-tuple-element.40), channel_id=1, source_target_pairs={{0,1},{1,0},{2,3},{3,2},{4,5},{5,4},{6,7},{7,6},{8,9},{9,8},{10,11... | collective-permute-start | bytes 589832 | tf_op jit(solution)/shard_map/ppermute | solution.py:428
  15.7 4.8 %collective-permute-start.3 = (f32[8,128]{1,0:T(8,128)S(1)}, f32[8,128]{1,0:T(8,128)S(1)}, u32[]{:S(2)}, u32[]{:S(2)}) collective-permute-start(f32[8,128]{1,0:T(8,128)S(1)} %maximum_maximum_fusion.1.dep), channel_id=1, source_target_pairs={{1,12},{5,14},{9,10},{13,6},{15,2},{11,0},{7,4},{3,8},{12,1},{14,5... | collective-permute-start | bytes 12296 | tf_op jit(solution)/shard_map/ppermute | solution.py:428
  20.6 1.2 %collective-permute-start.6 = (f32[8,128]{1,0:T(8,128)S(1)}, f32[8,128]{1,0:T(8,128)S(1)}, u32[]{:S(2)}, u32[]{:S(2)}) collective-permute-start(f32[8,128]{1,0:T(8,128)S(1)} %maximum_maximum_fusion.mine), channel_id=1, source_target_pairs={{0,1},{1,0},{2,3},{3,2},{4,5},{5,4},{6,7},{7,6},{8,9},{9,8},{10,11... | collective-permute-start | bytes 12296 | tf_op jit(solution)/shard_map/ppermute | solution.py:428
  22.2 8.1 %collective-permute-start.7 = (f32[3,64,256]{2,1,0:T(8,128)S(1)}, f32[3,64,256]{2,1,0:T(8,128)S(1)}, u32[]{:S(2)}, u32[]{:S(2)}) collective-permute-start(f32[3,64,256]{2,1,0:T(8,128)S(1)} %get-tuple-element.51), channel_id=1, source_target_pairs={{0,1},{1,0},{2,3},{3,2},{4,5},{5,4},{6,7},{7,6},{8,9},{9,8},{10,11... | collective-permute-start | bytes 589832 | tf_op jit(solution)/shard_map/ppermute | solution.py:428
  22.5 7.8 %collective-permute-start.8 = (f32[3,64,256]{2,1,0:T(8,128)S(1)}, f32[3,64,256]{2,1,0:T(8,128)S(1)}, u32[]{:S(2)}, u32[]{:S(2)}) collective-permute-start(f32[3,64,256]{2,1,0:T(8,128)S(1)} %get-tuple-element.52), channel_id=1, source_target_pairs={{1,2},{3,4},{5,6},{7,8},{9,10},{11,12},{13,14},{15,0},{2,1},{4,3},... | collective-permute-start | bytes 589832 | tf_op jit(solution)/shard_map/ppermute | solution.py:428
  32.7 8.4 %collective-permute-start.9 = (f32[3,64,256]{2,1,0:T(8,128)S(1)}, f32[3,64,256]{2,1,0:T(8,128)S(1)}, u32[]{:S(2)}, u32[]{:S(2)}) collective-permute-start(f32[3,64,256]{2,1,0:T(8,128)S(1)} %get-tuple-element.57), channel_id=1, source_target_pairs={{0,1},{1,0},{2,3},{3,2},{4,5},{5,4},{6,7},{7,6},{8,9},{9,8},{10,11... | collective-permute-start | bytes 589832 | tf_op jit(solution)/shard_map/ppermute | solution.py:428
  32.8 8.3 %collective-permute-start.10 = (f32[3,64,256]{2,1,0:T(8,128)S(1)}, f32[3,64,256]{2,1,0:T(8,128)S(1)}, u32[]{:S(2)}, u32[]{:S(2)}) collective-permute-start(f32[3,64,256]{2,1,0:T(8,128)S(1)} %get-tuple-element.58), channel_id=1, source_target_pairs={{1,2},{3,4},{5,6},{7,8},{9,10},{11,12},{13,14},{15,0},{2,1},{4,3},... | collective-permute-start | bytes 589832 | tf_op jit(solution)/shard_map/ppermute | solution.py:428
